TPU v7x, 128 devices: a whole 4x4x4 slice. The times are simulated.
128 devices in a mesh: grp: 8 (over x, core), sub: 16 (over z, y).
Axes of the slice: x: 4, y: 4, z: 4, core: 2. Of those that a mesh axis runs over, the one named last changes fastest.
Arguments:
- bg_vel: float32 [3, 64, 256, 256], P(None, 'grp', 'sub'), may hold values from -6 to 6
- nb_vel: float32 [3, 64, 256, 256], P(None, 'grp', 'sub'), may hold values from -6 to 6
- bg_source: float32 [3, 64, 256, 256], P(None, 'grp', 'sub'), may hold values from -6 to 6
- nb_source: float32 [3, 64, 256, 256], P(None, 'grp', 'sub'), may hold values from -6 to 6
- bg_inertia: float32 [64, 256, 256], P('grp', 'sub'), may hold values from 0.5 to 4
- nb_inertia: float32 [64, 256, 256], P('grp', 'sub'), may hold values from 0.5 to 4
- bg_donor_cells: int32 [128, 128, 128], P(('grp', 'sub')), may hold values from 0 to 28414, as said below
- bg_donor_weights: float32 [128, 128, 8, 128], P(('grp', 'sub')), may hold values from 0 to 1, as said below
- nb_donor_cells: int32 [128, 128, 128], P(('grp', 'sub')), may hold values from 0 to 28414, as said below
- nb_donor_weights: float32 [128, 128, 8, 128], P(('grp', 'sub')), may hold values from 0 to 1, as said below
- nb_receptors: int32 [128, 128, 128], P(('grp', 'sub')), may hold values from -1 to 30719, as said below
- bg_receptors: int32 [128, 128, 128], P(('grp', 'sub')), may hold values from -1 to 30719, as said below
Outputs:
- bg_out: float32 [3, 64, 256, 256], P(None, 'grp', 'sub')
- nb_out: float32 [3, 64, 256, 256], P(None, 'grp', 'sub')
Inputs may be any that keep to these rules, and one draw needn't show every extreme that they name: `bg_donor_cells`: every base cell has streamwise, spanwise and vertical coordinates below 7, 15 and 255, so that its eight corners lie in the donor's block. `nb_donor_cells`: as for bg_donor_cells. `bg_donor_weights`: the eight weights of a slot are non-negative and sum to one. `nb_donor_weights`: as for bg_donor_weights. `nb_receptors`: live entries are flat cell indices into the receiving device's block. The live cells of one receiving device are distinct; for each donor device the live slots come first and number at least 32; on every receiving device some donor device fills all 128 slots. `bg_receptors`: as for nb_receptors.
All inputs are finite; a program needn't handle non-finite values.
Results may differ from a plain program's by a relative error of at most 0.0003.
Values sent between devices are 32-bit elements; how exact they have to be, the bound alone decides.
A program may use at most 256 MiB of HBM per device.

v0:
```python
import jax
import jax.numpy as jnp
from jax import lax
from jax.sharding import PartitionSpec as P

SWEEPS = 4


def extended(block, sides, width):
    for axis, dim in sides:
        count = lax.axis_size(axis)
        forward = [(i, i + 1) for i in range(count - 1)]
        backward = [(target, source) for source, target in forward]
        low = lax.ppermute(
            lax.slice_in_dim(block, block.shape[dim] - width, None, axis=dim), axis, forward
        )
        high = lax.ppermute(lax.slice_in_dim(block, 0, width, axis=dim), axis, backward)
        block = jnp.concatenate([low, block, high], axis=dim)
    return block


def stencil_offsets(rows_y, rows_z):
    return jnp.array(
        [
            step_x * rows_y * rows_z + step_y * rows_z + step_z
            for step_x in (0, 1)
            for step_y in (0, 1)
            for step_z in (0, 1)
        ],
        jnp.int32,
    )


def interpolate(flat_field, base_cells, weights, offsets_table):
    indices = base_cells[:, None, :] + offsets_table[None, :, None]
    values = flat_field[:, indices]
    return jnp.sum(values * weights[None], axis=2)


def overwrite(flat_field, receptors, values):
    cells_total = flat_field.shape[1]
    indices = jnp.where(receptors < 0, cells_total, receptors).reshape(-1)
    updated = flat_field.at[:, indices].set(values.reshape(values.shape[0], -1), mode="drop")
    frozen = jnp.zeros((1, cells_total), jnp.float32).at[:, indices].set(1.0, mode="drop")
    return (updated, frozen)


def cell_faces(padded):
    middle = padded[..., 1:-1, 1:-1, 1:-1]
    after_cells = (
        padded[..., 2:, 1:-1, 1:-1],
        padded[..., 1:-1, 2:, 1:-1],
        padded[..., 1:-1, 1:-1, 2:],
    )
    before_cells = (
        padded[..., :-2, 1:-1, 1:-1],
        padded[..., 1:-1, :-2, 1:-1],
        padded[..., 1:-1, 1:-1, :-2],
    )
    return (middle, after_cells, before_cells)


def assemble(padded, inertia):
    middle, after_cells, before_cells = cell_faces(padded)
    coef_after = tuple(
        (
            1.0 + jax.nn.relu(-0.5 * (middle[direction] + after_cells[direction][direction]))
            for direction in range(3)
        )
    )
    coef_before = tuple(
        (
            1.0 + jax.nn.relu(0.5 * (middle[direction] + before_cells[direction][direction]))
            for direction in range(3)
        )
    )
    diagonal = inertia
    for direction in range(3):
        diagonal = diagonal + coef_after[direction] + coef_before[direction]
    return (coef_after, coef_before, diagonal)


def relax(padded, coef_after, coef_before, diagonal, right_side, frozen):
    middle, after_cells, before_cells = cell_faces(padded)
    summed = right_side
    for direction in range(3):
        summed = (
            summed
            + coef_after[direction] * after_cells[direction]
            + coef_before[direction] * before_cells[direction]
        )
    return jnp.where(frozen, middle, summed / diagonal)


def pad_background(velocity):
    padded = extended(velocity, (("grp", 1), ("sub", 2)), 1)
    return jnp.pad(padded, ((0, 0), (0, 0), (0, 0), (1, 1)))


def pad_nearbody(velocity):
    padded = extended(velocity, (("sub", 2),), 1)
    return jnp.pad(padded, ((0, 0), (1, 1), (0, 0), (1, 1)))


def solve_grid(start, source, inertia, frozen, padder):
    padded = padder(start)
    coef_after, coef_before, diagonal = assemble(padded, inertia)
    right_side = source + inertia * start
    velocity = start
    for sweep_index in range(SWEEPS):
        if sweep_index > 0:
            padded = padder(velocity)
        velocity = relax(padded, coef_after, coef_before, diagonal, right_side, frozen)
    return velocity


def body(
    bg_vel,
    nb_vel,
    bg_source,
    nb_source,
    bg_inertia,
    nb_inertia,
    bg_donor_cells,
    bg_donor_weights,
    nb_donor_cells,
    nb_donor_weights,
    nb_receptors,
    bg_receptors,
):
    comps, rows_x, rows_y, rows_z = bg_vel.shape
    offsets_table = stencil_offsets(rows_y, rows_z)
    bg_flat = bg_vel.reshape(comps, -1)
    nb_flat = nb_vel.reshape(comps, -1)
    to_near = interpolate(bg_flat, bg_donor_cells[0], bg_donor_weights[0], offsets_table)
    to_back = interpolate(nb_flat, nb_donor_cells[0], nb_donor_weights[0], offsets_table)
    got_near, got_back = (
        lax.all_to_all(to_near, ("grp", "sub"), split_axis=1, concat_axis=1, tiled=True),
        lax.all_to_all(to_back, ("grp", "sub"), split_axis=1, concat_axis=1, tiled=True),
    )
    nb_flat, nb_mask = overwrite(nb_flat, nb_receptors[0], got_near)
    bg_flat, bg_mask = overwrite(bg_flat, bg_receptors[0], got_back)
    local_shape = (rows_x, rows_y, rows_z)
    bg_start = bg_flat.reshape(bg_vel.shape)
    nb_start = nb_flat.reshape(nb_vel.shape)
    bg_out = solve_grid(
        bg_start, bg_source, bg_inertia, bg_mask.reshape(local_shape) > 0.5, pad_background
    )
    nb_out = solve_grid(
        nb_start, nb_source, nb_inertia, nb_mask.reshape(local_shape) > 0.5, pad_nearbody
    )
    return (bg_out, nb_out)


def solution(mesh):
    return jax.shard_map(
        body,
        mesh=mesh,
        in_specs=(
            P(None, "grp", "sub", None),
            P(None, "grp", "sub", None),
            P(None, "grp", "sub", None),
            P(None, "grp", "sub", None),
            P("grp", "sub", None),
            P("grp", "sub", None),
            P(("grp", "sub"), None, None),
            P(("grp", "sub"), None, None, None),
            P(("grp", "sub"), None, None),
            P(("grp", "sub"), None, None, None),
            P(("grp", "sub"), None, None),
            P(("grp", "sub"), None, None),
        ),
        out_specs=(P(None, "grp", "sub", None), P(None, "grp", "sub", None)),
        check_vma=False,
    )
```

profile of v0, /device:TPU:0, one launch (start us, length us, event | category | flops | bytes accessed | tf_op | source)
XLA Modules:
  0.0 1380.5 jit_solution(6825308085555568219)
XLA Ops:
  0.7 9.7 copy.81
  10.7 437.0 %gather_fusion.1 = f32[131072,3]{1,0:T(8,128)} fusion(f32[3,32768]{0,1:T(8,128)} %bitcast.194, s32[131072]{0:T(1024)S(1)} %get-tuple-element.66), kind=kCustom, calls=%fused_computation.1 | custom fusion | bytes 3670016 | tf_op jit(solution)/shard_map/gather | solution.py:36
  447.7 25.4 %multiply_reduce_fusion = f32[128,128,3]{2,1,0:T(8,128)} fusion(f32[128,8,128,3]{3,2,1,0:T(8,128)} %bitcast.28, f32[128,8,128]{2,1,0:T(8,128)S(1)} %bitcast.204), kind=kLoop, calls=%fused_computation.6 | loop fusion | flops 737280 | bytes 2293760 | tf_op jit(solution)/shard_map/reduce_sum | solution.py:37
  473.1 6.0 copy.92
  479.1 11.1 all-to-all-start.1
  490.3 8.6 copy.82
  499.0 60.4 %scatter_custom_fusion.2 = f32[32768]{0:T(1024)S(1)} fusion(s32[16384]{0:T(1024)S(1)} %bitcast.208, f32[16384]{0:T(1024)S(1)} %broadcast.224, f32[]{:T(128)} %constant.14.clone.1), kind=kCustom, calls=%fused_computation.290 | custom fusion | bytes 131076 | tf_op jit(solution)/shard_map/scatter | solution.py:44
  559.6 60.4 %scatter_custom_fusion = f32[32768]{0:T(1024)S(1)} fusion(s32[16384]{0:T(1024)S(1)} %bitcast.206, f32[16384]{0:T(1024)S(1)} %broadcast.224, f32[]{:T(128)} %constant.14.clone.1), kind=kCustom, calls=%fused_computation.292 | custom fusion | bytes 131076 | tf_op jit(solution)/shard_map/scatter | solution.py:44
  619.9 437.0 %gather_fusion = f32[131072,3]{1,0:T(8,128)} fusion(f32[3,32768]{0,1:T(8,128)} %bitcast.197, s32[131072]{0:T(1024)S(1)} %get-tuple-element.67), kind=kCustom, calls=%fused_computation | custom fusion | bytes 3670016 | tf_op jit(solution)/shard_map/gather | solution.py:36
  1057.0 25.5 %multiply_reduce_fusion.1 = f32[128,128,3]{2,1,0:T(8,128)} fusion(f32[128,8,128,3]{3,2,1,0:T(8,128)} %bitcast.6, f32[128,8,128]{2,1,0:T(8,128)S(1)} %bitcast.205), kind=kLoop, calls=%fused_computation.7 | loop fusion | flops 737280 | bytes 2293760 | tf_op jit(solution)/shard_map/reduce_sum | solution.py:37
  1082.5 5.9 copy.83
  1088.5 9.8 all-to-all-start
  1098.2 5.1 copy.93
  1103.3 52.2 %scatter_fusion.1 = f32[3,32768]{0,1:T(8,128)} fusion(f32[3,32768]{0,1:T(8,128)} %bitcast.198, s32[16384]{0:T(1024)S(1)} %bitcast.209, f32[16384,3]{1,0:T(8,128)} %copy.93), kind=kCustom, calls=%fused_computation.5 | custom fusion | bytes 655360 | tf_op jit(solution)/shard_map/scatter | solution.py:43
  1155.5 30.4 %slice_reduce_fusion.2 = (f32[32768]{0:T(1024)S(1)}, f32[32768]{0:T(1024)S(1)}, f32[32768]{0:T(1024)S(1)}) fusion(f32[3,32768]{0,1:T(8,128)} %scatter_fusion.1), kind=kLoop, calls=%fused_computation.10 | loop fusion | bytes 786432 | tf_op jit(solution)/shard_map/slice | solution.py:67
  1186.0 10.0 copy.100
  1196.0 2.9 collective-permute-start.16
  1200.2 5.1 copy.84
  1205.3 52.2 %scatter_fusion = f32[3,32768]{0,1:T(8,128)} fusion(f32[3,32768]{0,1:T(8,128)} %bitcast.195, s32[16384]{0:T(1024)S(1)} %bitcast.207, f32[16384,3]{1,0:T(8,128)} %copy.84), kind=kCustom, calls=%fused_computation.3 | custom fusion | bytes 655360 | tf_op jit(solution)/shard_map/scatter | solution.py:43
  1257.5 30.4 %slice_reduce_fusion.5 = (f32[32768]{0:T(1024)S(1)}, f32[32768]{0:T(1024)S(1)}, f32[32768]{0:T(1024)S(1)}) fusion(f32[3,32768]{0,1:T(8,128)} %scatter_fusion), kind=kLoop, calls=%fused_computation.13 | loop fusion | bytes 786432 | tf_op jit(solution)/shard_map/slice | solution.py:67
  1287.9 10.0 copy.91
  1299.8 3.0 collective-permute-start.1
  1305.1 4.5 collective-permute-start.18
  1312.4 5.2 collective-permute-start.3
  1322.7 3.0 collective-permute-start.5
  1325.8 4.2 collective-permute-start.20
  1332.7 5.2 collective-permute-start.7
  1342.3 3.0 collective-permute-start.9
  1347.5 6.5 collective-permute-start.11
  1354.1 6.3 collective-permute-start.22
  1364.1 3.5 collective-permute-start.13
  1370.2 7.0 collective-permute-start.15
  (116 shorter events, 32.6 us)
Async XLA Ops:
  0.6 9.7 copy-start.11
  0.6 9.7 copy-start.7
  10.7 437.0 %copy-start = (f32[1,128,8,128]{3,2,1,0:T(8,128)S(1)}, f32[1,128,8,128]{3,2,1,0:T(8,128)}, u32[]{:S(2)}) copy-start(f32[1,128,8,128]{3,2,1,0:T(8,128)} %param.20) | copy-start | bytes 1572868
  473.1 17.1 %copy-start.6 = (f32[3,8,16,256]{3,2,1,0:T(8,128)S(1)}, f32[3,8,16,256]{3,2,1,0:T(8,128)}, u32[]{:S(2)}) copy-start(f32[3,8,16,256]{3,2,1,0:T(8,128)} %param.14) | copy-start | bytes 1179652
  479.1 609.4 %all-to-all-start.1 = ((f32[3,128,128]{2,0,1:T(4,128)}), f32[3,128,128]{2,0,1:T(4,128)S(1)}, u32[]{:S(2)}, u32[]{:S(2)}) async-start(f32[3,128,128]{2,0,1:T(4,128)} %copy.92), calls=%async_computation.1 | async-start | bytes 524288 | tf_op jit(solution)/shard_map/all_to_all | solution.py:138
  490.3 69.2 %copy-start.10 = (s32[1,128,128]{2,1,0:T(8,128)S(1)}, s32[1,128,128]{2,1,0:T(8,128)}, u32[]{:S(2)}) copy-start(s32[1,128,128]{2,1,0:T(8,128)} %param.24) | copy-start | bytes 196612
  619.9 437.0 %copy-start.1 = (f32[1,128,8,128]{3,2,1,0:T(8,128)S(1)}, f32[1,128,8,128]{3,2,1,0:T(8,128)}, u32[]{:S(2)}) copy-start(f32[1,128,8,128]{3,2,1,0:T(8,128)} %param.22) | copy-start | bytes 1572868
  1088.5 111.7 %all-to-all-start = ((f32[3,128,128]{2,0,1:T(4,128)}), f32[3,128,128]{2,0,1:T(4,128)S(1)}, u32[]{:S(2)}, u32[]{:S(2)}) async-start(f32[3,128,128]{2,0,1:T(4,128)} %copy.83), calls=%async_computation | async-start | bytes 524288 | tf_op jit(solution)/shard_map/all_to_all | solution.py:139
  1196.0 106.8 %collective-permute-start.16 = (f32[3,8,1,256]{3,2,1,0:T(1,128)S(1)}, f32[3,8,1,256]{3,2,1,0:T(1,128)S(1)}, u32[]{:S(2)}, u32[]{:S(2)}) collective-permute-start(f32[3,8,1,256]{3,2,1,0:T(1,128)S(1)} %get-tuple-element.56), channel_id=1, source_target_pairs={{0,1},{1,2},{2,3},{3,4},{4,5},{5,6},{6,7},{7,8},{8,9},{9,10},{10,1... | collective-permute-start | bytes 73736 | tf_op jit(solution)/shard_map/ppermute | solution.py:14
  1198.9 103.9 %collective-permute-start.17 = (f32[3,8,1,256]{3,2,1,0:T(1,128)S(1)}, f32[3,8,1,256]{3,2,1,0:T(1,128)S(1)}, u32[]{:S(2)}, u32[]{:S(2)}) collective-permute-start(f32[3,8,1,256]{3,2,1,0:T(1,128)S(1)} %get-tuple-element.57), channel_id=1, source_target_pairs={{1,0},{2,1},{3,2},{4,3},{5,4},{6,5},{7,6},{8,7},{9,8},{10,9},{11,1... | collective-permute-start | bytes 73736 | tf_op jit(solution)/shard_map/ppermute | solution.py:17
  1298.5 12.5 collective-permute-start
  1299.8 11.2 collective-permute-start.1
  1305.1 12.4 collective-permute-start.18
  1309.7 7.9 collective-permute-start.19
  1311.1 7.5 collective-permute-start.2
  1312.4 6.7 collective-permute-start.3
  1321.4 9.9 collective-permute-start.4
  1322.7 8.6 collective-permute-start.5
  1325.8 12.1 collective-permute-start.20
  1330.1 7.9 collective-permute-start.21
  1331.4 7.0 collective-permute-start.6
  1332.7 6.9 collective-permute-start.7
  1340.7 5.1 collective-permute-start.8
  1342.3 3.9 collective-permute-start.9
  1346.2 15.5 %collective-permute-start.10 = (f32[3,10,1,256]{3,2,1,0:T(1,128)S(1)}, f32[3,10,1,256]{3,2,1,0:T(1,128)S(1)}, u32[]{:S(2)}, u32[]{:S(2)}) collective-permute-start(f32[3,10,1,256]{3,2,1,0:T(1,128)S(1)} %get-tuple-element.45), channel_id=1, source_target_pairs={{1,0},{2,1},{3,2},{4,3},{5,4},{6,5},{7,6},{8,7},{9,8},{10,9},{11,1... | collective-permute-start | bytes 92168 | tf_op jit(solution)/shard_map/ppermute | solution.py:17
  1347.5 14.2 %collective-permute-start.11 = (f32[3,10,1,256]{3,2,1,0:T(1,128)S(1)}, f32[3,10,1,256]{3,2,1,0:T(1,128)S(1)}, u32[]{:S(2)}, u32[]{:S(2)}) collective-permute-start(f32[3,10,1,256]{3,2,1,0:T(1,128)S(1)} %get-tuple-element.44), channel_id=1, source_target_pairs={{0,1},{1,2},{2,3},{3,4},{4,5},{5,6},{6,7},{7,8},{8,9},{9,10},{10,1... | collective-permute-start | bytes 92168 | tf_op jit(solution)/shard_map/ppermute | solution.py:14
  1354.1 13.5 collective-permute-start.22
  1360.4 7.9 collective-permute-start.23
  1362.8 6.0 collective-permute-start.12
  1364.1 4.7 collective-permute-start.13
  1368.9 9.5 collective-permute-start.14
  1370.2 8.5 collective-permute-start.15
  (6 other events, 22.2 us)
where the time goes:
time: 1390 us; the launch traced here: 1380 us
  local copies, waits for them, and re-layouts  1220 us (88%)
  starting transfers between devices  91 us (7%)
  other arithmetic  62.3 us (4%)
    gather x2, local copies, waits for them, and re-layouts, interpolate(): values = flat_field[:, indices]  874 us
    scatter x2, local copies, waits for them, and re-layouts, overwrite(): jnp.zeros((1, cells_total), jnp.float32).at[:, indices]  121 us
    scatter x2, local copies, waits for them, and re-layouts, overwrite(): flat_field.at[:, indices]  104 us
    slice x3, local copies, waits for them, and re-layouts, assemble(): middle[direction] + after_cells[direction][direction]  60.9 us
    ppermute x12, starting transfers between devices, extended(): lax.ppermute(lax.slice_in_dim(block, block.shape[dim] - width, None, axis...  54.4 us
    reduce_sum x2, other arithmetic, interpolate(): return jnp.sum(values * weights[None], axis=2)  50.9 us
  transfers between devices with their start and end apart: 26, of which 5 were waited for; matrix products, arithmetic and copies ran while one was open for 58% of the time, Pallas kernels for 0%

commit v1 on v0

--- a/solution.py
+++ b/solution.py
@@ -1,7 +1,158 @@
 import jax
 import jax.numpy as jnp
 from jax import lax
+from jax.experimental import pallas as pl
+from jax.experimental.pallas import tpu as pltpu
 from jax.sharding import PartitionSpec as P
+
+BF = jnp.bfloat16
+F32 = jnp.float32
+
+
+def split(x):
+    hi = x.astype(BF)
+    lo = (x - hi.astype(F32)).astype(BF)
+    return hi, lo
+
+
+def interp_one(field, cells, weights, out, table, base):
+    x = field[...].reshape(384, 256)
+    hi, lo = split(x)
+    table[0:384, :] = hi
+    table[768:1152, :] = lo
+    hi, lo = split(pltpu.roll(x, 255, 1))
+    table[384:768, :] = hi
+    table[1152:1536, :] = lo
+    z_iota = lax.broadcasted_iota(jnp.int32, (256, 128), 0).astype(F32).astype(BF)
+    y_iota = lax.broadcasted_iota(jnp.int32, (16, 128), 0)
+
+    def step(i, carry):
+        tile = cells[0, pl.ds(pl.multiple_of(i * 8, 8), 8), :]
+        z_tile = (tile & 255).astype(F32).astype(BF)
+        y_tile = (tile >> 8) & 15
+        x_tile = tile >> 12
+        for pair in range(4):
+            hot = [
+                jnp.where(z_iota == z_tile[s : s + 1, :], jnp.ones((), BF), jnp.zeros((), BF))
+                for s in (2 * pair, 2 * pair + 1)
+            ]
+            hot = jnp.concatenate(hot, axis=1)
+            got = jnp.dot(table[0:768, :], hot, preferred_element_type=F32)
+            got = got + jnp.dot(table[768:1536, :], hot, preferred_element_type=F32)
+            for half in range(2):
+                s = 2 * pair + half
+                r = i * 8 + s
+                w = weights[0, r]
+                y_row = y_tile[s : s + 1, :]
+                x_row = jnp.broadcast_to(x_tile[s : s + 1, :], (16, 128))
+                y_here = y_iota == y_row
+                y_next = y_iota == y_row + 1
+                by_y = {}
+                for a in range(2):
+                    for zc in range(2):
+                        k = 4 * a + zc
+                        by_y[a, zc] = jnp.where(
+                            y_here, w[k : k + 1, :], jnp.where(y_next, w[k + 2 : k + 3, :], 0.0)
+                        )
+                acc = [None] * 3
+                before = None
+                for xx in range(8):
+                    here = x_row == xx if xx < 7 else None
+                    for zc in range(2):
+                        coef = None
+                        if before is not None:
+                            coef = jnp.where(before, by_y[1, zc], 0.0)
+                        if here is not None:
+                            coef = jnp.where(here, by_y[0, zc], 0.0 if coef is None else coef)
+                        for c in range(3):
+                            at = zc * 384 + c * 128 + xx * 16
+                            term = coef * got[at : at + 16, half * 128 : half * 128 + 128]
+                            acc[c] = term if acc[c] is None else acc[c] + term
+                    before = here
+                for c in range(3):
+                    out[r, base + c, :] = jnp.sum(acc[c], axis=0)
+        return carry
+
+    lax.fori_loop(0, 16, step, 0)
+
+
+def interp_kernel(bg_vel, bg_cells, bg_w, nb_vel, nb_cells, nb_w, out, table):
+    interp_one(bg_vel, bg_cells, bg_w, out, table, 0)
+    interp_one(nb_vel, nb_cells, nb_w, out, table, 3)
+
+
+def interpolate(*args):
+    return pl.pallas_call(
+        interp_kernel,
+        out_shape=jax.ShapeDtypeStruct((128, 8, 128), F32),
+        in_specs=[pl.BlockSpec(memory_space=pltpu.VMEM)] * 6,
+        out_specs=pl.BlockSpec(memory_space=pltpu.VMEM),
+        scratch_shapes=[pltpu.VMEM((1536, 256), BF)],
+        compiler_params=pltpu.CompilerParams(vmem_limit_bytes=40 * 2**20),
+        name="interpolate",
+    )(*args)
+
+
+def scatter_one(field, receptors, got, base, start, frozen, left, total):
+    z_iota = lax.broadcasted_iota(jnp.int32, (256, 128), 0).astype(F32).astype(BF)
+    r_iota = lax.broadcasted_iota(jnp.int32, (128, 128), 0).astype(F32).astype(BF)
+    one = jnp.ones((), BF)
+    zero = jnp.zeros((), BF)
+    total[...] = jnp.zeros_like(total)
+
+    def step(i, carry):
+        tile = receptors[0, pl.ds(pl.multiple_of(i * 8, 8), 8), :]
+        z_tile = (tile & 255).astype(F32).astype(BF)
+        r_tile = (tile >> 8).astype(F32).astype(BF)
+        hots = []
+        for s in range(8):
+            hots.append(jnp.where(z_iota == z_tile[s : s + 1, :], one, zero))
+            mine = r_iota == r_tile[s : s + 1, :]
+            values = got[i * 8 + s]
+            hi, lo = split(values)
+            for c in range(3):
+                left[c * 128 : c * 128 + 128, s * 128 : s * 128 + 128] = jnp.where(
+                    mine, hi[base + c : base + c + 1, :], zero
+                )
+                left[384 + c * 128 : 512 + c * 128, s * 128 : s * 128 + 128] = jnp.where(
+                    mine, lo[base + c : base + c + 1, :], zero
+                )
+            left[768:896, s * 128 : s * 128 + 128] = jnp.where(mine, one, zero)
+        hot = jnp.concatenate(hots, axis=1)
+        total[...] += lax.dot_general(
+            left[...], hot, (((1,), (1,)), ((), ())), preferred_element_type=F32
+        )
+        return carry
+
+    lax.fori_loop(0, 16, step, 0)
+    mask = total[768:896, :]
+    frozen[...] = mask.reshape(8, 16, 256)
+    for c in range(3):
+        value = total[c * 128 : c * 128 + 128, :] + total[384 + c * 128 : 512 + c * 128, :]
+        old = field[c].reshape(128, 256)
+        start[c] = jnp.where(mask > 0.5, value, old).reshape(8, 16, 256)
+
+
+def scatter_kernel(
+    got, nb_rec, bg_rec, nb_vel, bg_vel, nb_start, nb_frozen, bg_start, bg_frozen, left, total
+):
+    scatter_one(nb_vel, nb_rec, got, 0, nb_start, nb_frozen, left, total)
+    scatter_one(bg_vel, bg_rec, got, 3, bg_start, bg_frozen, left, total)
+
+
+def overwrite(*args):
+    field = jax.ShapeDtypeStruct((3, 8, 16, 256), F32)
+    mask = jax.ShapeDtypeStruct((8, 16, 256), F32)
+    return pl.pallas_call(
+        scatter_kernel,
+        out_shape=(field, mask, field, mask),
+        in_specs=[pl.BlockSpec(memory_space=pltpu.VMEM)] * 5,
+        out_specs=[pl.BlockSpec(memory_space=pltpu.VMEM)] * 4,
+        scratch_shapes=[pltpu.VMEM((896, 1024), BF), pltpu.VMEM((896, 256), F32)],
+        compiler_params=pltpu.CompilerParams(vmem_limit_bytes=40 * 2**20),
+        name="overwrite",
+    )(*args)
+
 
 SWEEPS = 4
 
@@ -17,32 +168,6 @@
         high = lax.ppermute(lax.slice_in_dim(block, 0, width, axis=dim), axis, backward)
         block = jnp.concatenate([low, block, high], axis=dim)
     return block
-
-
-def stencil_offsets(rows_y, rows_z):
-    return jnp.array(
-        [
-            step_x * rows_y * rows_z + step_y * rows_z + step_z
-            for step_x in (0, 1)
-            for step_y in (0, 1)
-            for step_z in (0, 1)
-        ],
-        jnp.int32,
-    )
-
-
-def interpolate(flat_field, base_cells, weights, offsets_table):
-    indices = base_cells[:, None, :] + offsets_table[None, :, None]
-    values = flat_field[:, indices]
-    return jnp.sum(values * weights[None], axis=2)
-
-
-def overwrite(flat_field, receptors, values):
-    cells_total = flat_field.shape[1]
-    indices = jnp.where(receptors < 0, cells_total, receptors).reshape(-1)
-    updated = flat_field.at[:, indices].set(values.reshape(values.shape[0], -1), mode="drop")
-    frozen = jnp.zeros((1, cells_total), jnp.float32).at[:, indices].set(1.0, mode="drop")
-    return (updated, frozen)
 
 
 def cell_faces(padded):
@@ -128,26 +253,14 @@
     nb_receptors,
     bg_receptors,
 ):
-    comps, rows_x, rows_y, rows_z = bg_vel.shape
-    offsets_table = stencil_offsets(rows_y, rows_z)
-    bg_flat = bg_vel.reshape(comps, -1)
-    nb_flat = nb_vel.reshape(comps, -1)
-    to_near = interpolate(bg_flat, bg_donor_cells[0], bg_donor_weights[0], offsets_table)
-    to_back = interpolate(nb_flat, nb_donor_cells[0], nb_donor_weights[0], offsets_table)
-    got_near, got_back = (
-        lax.all_to_all(to_near, ("grp", "sub"), split_axis=1, concat_axis=1, tiled=True),
-        lax.all_to_all(to_back, ("grp", "sub"), split_axis=1, concat_axis=1, tiled=True),
-    )
-    nb_flat, nb_mask = overwrite(nb_flat, nb_receptors[0], got_near)
-    bg_flat, bg_mask = overwrite(bg_flat, bg_receptors[0], got_back)
-    local_shape = (rows_x, rows_y, rows_z)
-    bg_start = bg_flat.reshape(bg_vel.shape)
-    nb_start = nb_flat.reshape(nb_vel.shape)
+    sent = interpolate(bg_vel, bg_donor_cells, bg_donor_weights, nb_vel, nb_donor_cells, nb_donor_weights)
+    got = lax.all_to_all(sent, ("grp", "sub"), split_axis=0, concat_axis=0, tiled=True)
+    nb_start, nb_mask, bg_start, bg_mask = overwrite(got, nb_receptors, bg_receptors, nb_vel, bg_vel)
     bg_out = solve_grid(
-        bg_start, bg_source, bg_inertia, bg_mask.reshape(local_shape) > 0.5, pad_background
+        bg_start, bg_source, bg_inertia, bg_mask > 0.5, pad_background
     )
     nb_out = solve_grid(
-        nb_start, nb_source, nb_inertia, nb_mask.reshape(local_shape) > 0.5, pad_nearbody
+        nb_start, nb_source, nb_inertia, nb_mask > 0.5, pad_nearbody
     )
     return (bg_out, nb_out)
 

time: 1390 us -> 190 us (0.14)
  the two profiles are of different devices: /device:TPU:0 before, /device:TPU:34 now
where the time goes in v1:
time: 190 us; the launch traced here: 189 us
  starting transfers between devices  73.9 us (39%)
  Pallas kernels  59.1 us (31%)
  blocking collectives  22.5 us (12%)
  waiting for transfers between devices  14.1 us (7%)
  other arithmetic  10.4 us (5%)
  local copies, waits for them, and re-layouts  8.01 us (4%)
    ppermute x12, starting transfers between devices, extended(): lax.ppermute(lax.slice_in_dim(block, 0, width, axis=dim), axis, backward)  40.8 us
    pallas_call x1, Pallas kernels, interpolate(): pl.pallas_call(interp_kernel, out_shape=jax.ShapeDtypeStruct((128, 8, 128...  36.4 us
    ppermute x12, starting transfers between devices, extended(): lax.ppermute(lax.slice_in_dim(block, block.shape[dim] - width, None, axis...  33.1 us
    pallas_call x1, Pallas kernels, overwrite(): pl.pallas_call(scatter_kernel, out_shape=(field, mask, field, mask), in_s...  22.7 us
    all_to_all x1, blocking collectives, body(): lax.all_to_all(sent, ('grp', 'sub'), split_axis=0, concat_axis=0, tiled=T...  22.5 us
    ppermute x12, waiting for transfers between devices, extended(): lax.ppermute(lax.slice_in_dim(block, block.shape[dim] - width, None, axis...  14 us
    unnamed x29, local copies, waits for them, and re-layouts  7.65 us
    select_n x8, other arithmetic, relax(): return jnp.where(frozen, middle, summed / diagonal)  5.48 us
  transfers between devices with their start and end apart: 24, of which 5 were waited for; matrix products, arithmetic and copies ran while one was open for 3% of the time, Pallas kernels for 0%

profile of v1, /device:TPU:34, one launch (start us, length us, event | category | flops | bytes accessed | tf_op | source)
XLA Modules:
  0.0 189.3 jit_solution(6600964380786415815)
XLA Ops:
  6.4 36.4 %interpolate.1 = f32[128,8,128]{2,1,0:T(8,128)S(1)} custom-call(f32[3,8,16,256]{3,2,1,0:T(8,128)S(1)} %copy-done, s32[1,128,128]{2,1,0:T(8,128)S(1)} %copy-done.5, f32[1,128,8,128]{3,2,1,0:T(8,128)S(1)} %copy-done.3, f32[3,8,16,256]{3,2,1,0:T(8,128)S(1)} %copy-done.1, s32[1,128,128]{2,1,0:T(8,128)S(1)} %copy-done.6, f32[1,128,8,128]{3,2,1,0:T(8,128)S(1)} %copy-done.4), custom_call_target="tpu_custom_call" | custom-call | tf_op jit(solution)/shard_map/interpolate/pallas_call | solution.py:85
  42.8 22.5 %all_to_all.5.got = f32[128,8,128]{2,1,0:T(8,128)S(1)} all-to-all(f32[128,8,128]{2,1,0:T(8,128)S(1)} %interpolate.1), channel_id=1, replica_groups=mesh['grp'=8,'sub'=16] {'grp','sub'}, dimensions={0} | all-to-all | bytes 1048576 | tf_op jit(solution)/shard_map/all_to_all | solution.py:257
  65.4 22.7 %overwrite.1 = (f32[3,8,16,256]{3,2,1,0:T(8,128)S(1)}, f32[8,16,256]{2,1,0:T(8,128)S(1)}, f32[3,8,16,256]{3,2,1,0:T(8,128)S(1)}, f32[8,16,256]{2,1,0:T(8,128)S(1)}) custom-call(f32[128,8,128]{2,1,0:T(8,128)S(1)} %all_to_all.5.got, s32[1,128,128]{2,1,0:T(8,128)S(1)} %copy-done.7, s32[1,128,128]{2,1,0:T(8,128)S(1)} %copy-done.8, ...), custom_call_target="tpu_custom_call" | custom-call | tf_op jit(solution)/shard_map/overwrite/pallas_call | solution.py:146
  88.1 2.5 %collective-permute-start.16 = (f32[3,8,1,256]{3,2,1,0:T(1,128)S(1)}, f32[3,8,1,256]{3,2,1,0:T(1,128)S(1)}, u32[]{:S(2)}, u32[]{:S(2)}) collective-permute-start(f32[3,8,1,256]{3,2,1,0:T(1,128)S(1)} %get-tuple-element.42), channel_id=1, source_target_pairs={{0,1},{1,2},{2,3},{3,4},{4,5},{5,6},{6,7},{7,8},{8,9},{9,10},{10,1... | collective-permute-start | bytes 73736 | tf_op jit(solution)/shard_map/ppermute | solution.py:165
  90.7 5.4 %collective-permute-start.17 = (f32[3,8,1,256]{3,2,1,0:T(1,128)S(1)}, f32[3,8,1,256]{3,2,1,0:T(1,128)S(1)}, u32[]{:S(2)}, u32[]{:S(2)}) collective-permute-start(f32[3,8,1,256]{3,2,1,0:T(1,128)S(1)} %get-tuple-element.43), channel_id=1, source_target_pairs={{1,0},{2,1},{3,2},{4,3},{5,4},{6,5},{7,6},{8,7},{9,8},{10,9},{11,1... | collective-permute-start | bytes 73736 | tf_op jit(solution)/shard_map/ppermute | solution.py:168
  96.1 1.9 %collective-permute-start.1 = (f32[3,1,16,256]{3,2,1,0:T(8,128)S(1)}, f32[3,1,16,256]{3,2,1,0:T(8,128)S(1)}, u32[]{:S(2)}, u32[]{:S(2)}) collective-permute-start(f32[3,1,16,256]{3,2,1,0:T(8,128)S(1)} %get-tuple-element.54), channel_id=1, source_target_pairs={{0,16},{16,32},{32,48},{48,64},{64,80},{80,96},{96,112},{1,17},{17... | collective-permute-start | bytes 147464 | tf_op jit(solution)/shard_map/ppermute | solution.py:165
  98.0 3.6 %collective-permute-start = (f32[3,1,16,256]{3,2,1,0:T(8,128)S(1)}, f32[3,1,16,256]{3,2,1,0:T(8,128)S(1)}, u32[]{:S(2)}, u32[]{:S(2)}) collective-permute-start(f32[3,1,16,256]{3,2,1,0:T(8,128)S(1)} %get-tuple-element.53), channel_id=1, source_target_pairs={{16,0},{32,16},{48,32},{64,48},{80,64},{96,80},{112,96},{17,1},{33... | collective-permute-start | bytes 147464 | tf_op jit(solution)/shard_map/ppermute | solution.py:168
  104.2 1.9 %collective-permute-start.18 = (f32[3,8,1,256]{3,2,1,0:T(1,128)S(1)}, f32[3,8,1,256]{3,2,1,0:T(1,128)S(1)}, u32[]{:S(2)}, u32[]{:S(2)}) collective-permute-start(f32[3,8,1,256]{3,2,1,0:T(1,128)S(1)} %get-tuple-element.40), channel_id=1, source_target_pairs={{0,1},{1,2},{2,3},{3,4},{4,5},{5,6},{6,7},{7,8},{8,9},{9,10},{10,1... | collective-permute-start | bytes 73736 | tf_op jit(solution)/shard_map/ppermute | solution.py:165
  106.2 6.0 %collective-permute-start.19 = (f32[3,8,1,256]{3,2,1,0:T(1,128)S(1)}, f32[3,8,1,256]{3,2,1,0:T(1,128)S(1)}, u32[]{:S(2)}, u32[]{:S(2)}) collective-permute-start(f32[3,8,1,256]{3,2,1,0:T(1,128)S(1)} %get-tuple-element.41), channel_id=1, source_target_pairs={{1,0},{2,1},{3,2},{4,3},{5,4},{6,5},{7,6},{8,7},{9,8},{10,9},{11,1... | collective-permute-start | bytes 73736 | tf_op jit(solution)/shard_map/ppermute | solution.py:168
  112.4 1.9 %collective-permute-start.2 = (f32[3,10,1,256]{3,2,1,0:T(1,128)S(1)}, f32[3,10,1,256]{3,2,1,0:T(1,128)S(1)}, u32[]{:S(2)}, u32[]{:S(2)}) collective-permute-start(f32[3,10,1,256]{3,2,1,0:T(1,128)S(1)} %get-tuple-element.35), channel_id=1, source_target_pairs={{1,0},{2,1},{3,2},{4,3},{5,4},{6,5},{7,6},{8,7},{9,8},{10,9},{11,1... | collective-permute-start | bytes 92168 | tf_op jit(solution)/shard_map/ppermute | solution.py:168
  114.3 3.9 %collective-permute-start.3 = (f32[3,10,1,256]{3,2,1,0:T(1,128)S(1)}, f32[3,10,1,256]{3,2,1,0:T(1,128)S(1)}, u32[]{:S(2)}, u32[]{:S(2)}) collective-permute-start(f32[3,10,1,256]{3,2,1,0:T(1,128)S(1)} %get-tuple-element.34), channel_id=1, source_target_pairs={{0,1},{1,2},{2,3},{3,4},{4,5},{5,6},{6,7},{7,8},{8,9},{9,10},{10,1... | collective-permute-start | bytes 92168 | tf_op jit(solution)/shard_map/ppermute | solution.py:165
  119.3 2.9 %collective-permute-done.3 = f32[3,10,1,256]{3,2,1,0:T(1,128)S(1)} collective-permute-done((f32[3,10,1,256]{3,2,1,0:T(1,128)S(1)}, f32[3,10,1,256]{3,2,1,0:T(1,128)S(1)}, u32[]{:S(2)}, u32[]{:S(2)}) %collective-permute-start.3) | collective-permute-done | bytes 30752 | tf_op jit(solution)/shard_map/ppermute | solution.py:165
  124.4 1.9 %collective-permute-start.4 = (f32[3,1,16,256]{3,2,1,0:T(8,128)S(1)}, f32[3,1,16,256]{3,2,1,0:T(8,128)S(1)}, u32[]{:S(2)}, u32[]{:S(2)}) collective-permute-start(f32[3,1,16,256]{3,2,1,0:T(8,128)S(1)} %get-tuple-element.49), channel_id=1, source_target_pairs={{16,0},{32,16},{48,32},{64,48},{80,64},{96,80},{112,96},{17,1},{33... | collective-permute-start | bytes 147464 | tf_op jit(solution)/shard_map/ppermute | solution.py:168
  126.3 2.4 %collective-permute-start.5 = (f32[3,1,16,256]{3,2,1,0:T(8,128)S(1)}, f32[3,1,16,256]{3,2,1,0:T(8,128)S(1)}, u32[]{:S(2)}, u32[]{:S(2)}) collective-permute-start(f32[3,1,16,256]{3,2,1,0:T(8,128)S(1)} %get-tuple-element.48), channel_id=1, source_target_pairs={{0,16},{16,32},{32,48},{48,64},{64,80},{80,96},{96,112},{1,17},{17... | collective-permute-start | bytes 147464 | tf_op jit(solution)/shard_map/ppermute | solution.py:165
  128.8 1.9 %collective-permute-start.20 = (f32[3,8,1,256]{3,2,1,0:T(1,128)S(1)}, f32[3,8,1,256]{3,2,1,0:T(1,128)S(1)}, u32[]{:S(2)}, u32[]{:S(2)}) collective-permute-start(f32[3,8,1,256]{3,2,1,0:T(1,128)S(1)} %get-tuple-element.38), channel_id=1, source_target_pairs={{0,1},{1,2},{2,3},{3,4},{4,5},{5,6},{6,7},{7,8},{8,9},{9,10},{10,1... | collective-permute-start | bytes 73736 | tf_op jit(solution)/shard_map/ppermute | solution.py:165
  130.7 6.0 %collective-permute-start.21 = (f32[3,8,1,256]{3,2,1,0:T(1,128)S(1)}, f32[3,8,1,256]{3,2,1,0:T(1,128)S(1)}, u32[]{:S(2)}, u32[]{:S(2)}) collective-permute-start(f32[3,8,1,256]{3,2,1,0:T(1,128)S(1)} %get-tuple-element.39), channel_id=1, source_target_pairs={{1,0},{2,1},{3,2},{4,3},{5,4},{6,5},{7,6},{8,7},{9,8},{10,9},{11,1... | collective-permute-start | bytes 73736 | tf_op jit(solution)/shard_map/ppermute | solution.py:168
  136.8 1.9 %collective-permute-start.6 = (f32[3,10,1,256]{3,2,1,0:T(1,128)S(1)}, f32[3,10,1,256]{3,2,1,0:T(1,128)S(1)}, u32[]{:S(2)}, u32[]{:S(2)}) collective-permute-start(f32[3,10,1,256]{3,2,1,0:T(1,128)S(1)} %get-tuple-element.33), channel_id=1, source_target_pairs={{1,0},{2,1},{3,2},{4,3},{5,4},{6,5},{7,6},{8,7},{9,8},{10,9},{11,1... | collective-permute-start | bytes 92168 | tf_op jit(solution)/shard_map/ppermute | solution.py:168
  138.8 3.9 %collective-permute-start.7 = (f32[3,10,1,256]{3,2,1,0:T(1,128)S(1)}, f32[3,10,1,256]{3,2,1,0:T(1,128)S(1)}, u32[]{:S(2)}, u32[]{:S(2)}) collective-permute-start(f32[3,10,1,256]{3,2,1,0:T(1,128)S(1)} %get-tuple-element.32), channel_id=1, source_target_pairs={{0,1},{1,2},{2,3},{3,4},{4,5},{5,6},{6,7},{7,8},{8,9},{9,10},{10,1... | collective-permute-start | bytes 92168 | tf_op jit(solution)/shard_map/ppermute | solution.py:165
  143.2 3.4 %collective-permute-done.7 = f32[3,10,1,256]{3,2,1,0:T(1,128)S(1)} collective-permute-done((f32[3,10,1,256]{3,2,1,0:T(1,128)S(1)}, f32[3,10,1,256]{3,2,1,0:T(1,128)S(1)}, u32[]{:S(2)}, u32[]{:S(2)}) %collective-permute-start.7) | collective-permute-done | bytes 30752 | tf_op jit(solution)/shard_map/ppermute | solution.py:165
  147.7 1.9 %collective-permute-start.8 = (f32[3,1,16,256]{3,2,1,0:T(8,128)S(1)}, f32[3,1,16,256]{3,2,1,0:T(8,128)S(1)}, u32[]{:S(2)}, u32[]{:S(2)}) collective-permute-start(f32[3,1,16,256]{3,2,1,0:T(8,128)S(1)} %get-tuple-element.47), channel_id=1, source_target_pairs={{16,0},{32,16},{48,32},{64,48},{80,64},{96,80},{112,96},{17,1},{33... | collective-permute-start | bytes 147464 | tf_op jit(solution)/shard_map/ppermute | solution.py:168
  149.7 2.4 %collective-permute-start.9 = (f32[3,1,16,256]{3,2,1,0:T(8,128)S(1)}, f32[3,1,16,256]{3,2,1,0:T(8,128)S(1)}, u32[]{:S(2)}, u32[]{:S(2)}) collective-permute-start(f32[3,1,16,256]{3,2,1,0:T(8,128)S(1)} %get-tuple-element.46), channel_id=1, source_target_pairs={{0,16},{16,32},{32,48},{48,64},{64,80},{80,96},{96,112},{1,17},{17... | collective-permute-start | bytes 147464 | tf_op jit(solution)/shard_map/ppermute | solution.py:165
  152.6 2.5 %collective-permute-done.9 = f32[3,1,16,256]{3,2,1,0:T(8,128)S(1)} collective-permute-done((f32[3,1,16,256]{3,2,1,0:T(8,128)S(1)}, f32[3,1,16,256]{3,2,1,0:T(8,128)S(1)}, u32[]{:S(2)}, u32[]{:S(2)}) %collective-permute-start.9) | collective-permute-done | bytes 49184 | tf_op jit(solution)/shard_map/ppermute | solution.py:165
  155.1 1.9 %collective-permute-start.10 = (f32[3,10,1,256]{3,2,1,0:T(1,128)S(1)}, f32[3,10,1,256]{3,2,1,0:T(1,128)S(1)}, u32[]{:S(2)}, u32[]{:S(2)}) collective-permute-start(f32[3,10,1,256]{3,2,1,0:T(1,128)S(1)} %get-tuple-element.31), channel_id=1, source_target_pairs={{1,0},{2,1},{3,2},{4,3},{5,4},{6,5},{7,6},{8,7},{9,8},{10,9},{11,1... | collective-permute-start | bytes 92168 | tf_op jit(solution)/shard_map/ppermute | solution.py:168
  157.0 3.9 %collective-permute-start.11 = (f32[3,10,1,256]{3,2,1,0:T(1,128)S(1)}, f32[3,10,1,256]{3,2,1,0:T(1,128)S(1)}, u32[]{:S(2)}, u32[]{:S(2)}) collective-permute-start(f32[3,10,1,256]{3,2,1,0:T(1,128)S(1)} %get-tuple-element.30), channel_id=1, source_target_pairs={{0,1},{1,2},{2,3},{3,4},{4,5},{5,6},{6,7},{7,8},{8,9},{9,10},{10,1... | collective-permute-start | bytes 92168 | tf_op jit(solution)/shard_map/ppermute | solution.py:165
  161.0 1.9 %collective-permute-start.22 = (f32[3,8,1,256]{3,2,1,0:T(1,128)S(1)}, f32[3,8,1,256]{3,2,1,0:T(1,128)S(1)}, u32[]{:S(2)}, u32[]{:S(2)}) collective-permute-start(f32[3,8,1,256]{3,2,1,0:T(1,128)S(1)} %get-tuple-element.36), channel_id=1, source_target_pairs={{0,1},{1,2},{2,3},{3,4},{4,5},{5,6},{6,7},{7,8},{8,9},{9,10},{10,1... | collective-permute-start | bytes 73736 | tf_op jit(solution)/shard_map/ppermute | solution.py:165
  163.0 6.2 %collective-permute-start.23 = (f32[3,8,1,256]{3,2,1,0:T(1,128)S(1)}, f32[3,8,1,256]{3,2,1,0:T(1,128)S(1)}, u32[]{:S(2)}, u32[]{:S(2)}) collective-permute-start(f32[3,8,1,256]{3,2,1,0:T(1,128)S(1)} %get-tuple-element.37), channel_id=1, source_target_pairs={{1,0},{2,1},{3,2},{4,3},{5,4},{6,5},{7,6},{8,7},{9,8},{10,9},{11,1... | collective-permute-start | bytes 73736 | tf_op jit(solution)/shard_map/ppermute | solution.py:168
  170.2 1.9 %collective-permute-start.12 = (f32[3,1,16,256]{3,2,1,0:T(8,128)S(1)}, f32[3,1,16,256]{3,2,1,0:T(8,128)S(1)}, u32[]{:S(2)}, u32[]{:S(2)}) collective-permute-start(f32[3,1,16,256]{3,2,1,0:T(8,128)S(1)} %get-tuple-element.45), channel_id=1, source_target_pairs={{16,0},{32,16},{48,32},{64,48},{80,64},{96,80},{112,96},{17,1},{33... | collective-permute-start | bytes 147464 | tf_op jit(solution)/shard_map/ppermute | solution.py:168
  172.2 2.4 %collective-permute-start.13 = (f32[3,1,16,256]{3,2,1,0:T(8,128)S(1)}, f32[3,1,16,256]{3,2,1,0:T(8,128)S(1)}, u32[]{:S(2)}, u32[]{:S(2)}) collective-permute-start(f32[3,1,16,256]{3,2,1,0:T(8,128)S(1)} %get-tuple-element.44), channel_id=1, source_target_pairs={{0,16},{16,32},{32,48},{48,64},{64,80},{80,96},{96,112},{1,17},{17... | collective-permute-start | bytes 147464 | tf_op jit(solution)/shard_map/ppermute | solution.py:165
  175.1 2.5 %collective-permute-done.13 = f32[3,1,16,256]{3,2,1,0:T(8,128)S(1)} collective-permute-done((f32[3,1,16,256]{3,2,1,0:T(8,128)S(1)}, f32[3,1,16,256]{3,2,1,0:T(8,128)S(1)}, u32[]{:S(2)}, u32[]{:S(2)}) %collective-permute-start.13) | collective-permute-done | bytes 49184 | tf_op jit(solution)/shard_map/ppermute | solution.py:165
  177.6 1.9 %collective-permute-start.14 = (f32[3,10,1,256]{3,2,1,0:T(1,128)S(1)}, f32[3,10,1,256]{3,2,1,0:T(1,128)S(1)}, u32[]{:S(2)}, u32[]{:S(2)}) collective-permute-start(f32[3,10,1,256]{3,2,1,0:T(1,128)S(1)} %get-tuple-element.29), channel_id=1, source_target_pairs={{1,0},{2,1},{3,2},{4,3},{5,4},{6,5},{7,6},{8,7},{9,8},{10,9},{11,1... | collective-permute-start | bytes 92168 | tf_op jit(solution)/shard_map/ppermute | solution.py:168
  179.6 3.9 %collective-permute-start.15 = (f32[3,10,1,256]{3,2,1,0:T(1,128)S(1)}, f32[3,10,1,256]{3,2,1,0:T(1,128)S(1)}, u32[]{:S(2)}, u32[]{:S(2)}) collective-permute-start(f32[3,10,1,256]{3,2,1,0:T(1,128)S(1)} %get-tuple-element.28), channel_id=1, source_target_pairs={{0,1},{1,2},{2,3},{3,4},{4,5},{5,6},{6,7},{7,8},{8,9},{9,10},{10,1... | collective-permute-start | bytes 92168 | tf_op jit(solution)/shard_map/ppermute | solution.py:165
  184.8 2.7 %collective-permute-done.15 = f32[3,10,1,256]{3,2,1,0:T(1,128)S(1)} collective-permute-done((f32[3,10,1,256]{3,2,1,0:T(1,128)S(1)}, f32[3,10,1,256]{3,2,1,0:T(1,128)S(1)}, u32[]{:S(2)}, u32[]{:S(2)}) %collective-permute-start.15) | collective-permute-done | bytes 30752 | tf_op jit(solution)/shard_map/ppermute | solution.py:165
  (82 shorter events, 18.5 us)
Async XLA Ops:
  0.6 1.0 copy-start
  2.6 1.0 copy-start.3
  3.7 1.0 copy-start.4
  6.4 59.0 %copy-start.7 = (s32[1,128,128]{2,1,0:T(8,128)S(1)}, s32[1,128,128]{2,1,0:T(8,128)}, u32[]{:S(2)}) copy-start(s32[1,128,128]{2,1,0:T(8,128)} %nb_rec.1) | copy-start | bytes 196612
  6.4 59.0 %copy-start.8 = (s32[1,128,128]{2,1,0:T(8,128)S(1)}, s32[1,128,128]{2,1,0:T(8,128)}, u32[]{:S(2)}) copy-start(s32[1,128,128]{2,1,0:T(8,128)} %bg_rec.1) | copy-start | bytes 196612
  42.8 22.5 %copy-start.2 = (f32[3,8,16,256]{3,2,1,0:T(8,128)S(1)}, f32[3,8,16,256]{3,2,1,0:T(8,128)}, u32[]{:S(2)}) copy-start(f32[3,8,16,256]{3,2,1,0:T(8,128)} %nb_vel.3) | copy-start | bytes 1179652
  88.1 13.7 %collective-permute-start.16 = (f32[3,8,1,256]{3,2,1,0:T(1,128)S(1)}, f32[3,8,1,256]{3,2,1,0:T(1,128)S(1)}, u32[]{:S(2)}, u32[]{:S(2)}) collective-permute-start(f32[3,8,1,256]{3,2,1,0:T(1,128)S(1)} %get-tuple-element.42), channel_id=1, source_target_pairs={{0,1},{1,2},{2,3},{3,4},{4,5},{5,6},{6,7},{7,8},{8,9},{9,10},{10,1... | collective-permute-start | bytes 73736 | tf_op jit(solution)/shard_map/ppermute | solution.py:165
  90.7 11.1 %collective-permute-start.17 = (f32[3,8,1,256]{3,2,1,0:T(1,128)S(1)}, f32[3,8,1,256]{3,2,1,0:T(1,128)S(1)}, u32[]{:S(2)}, u32[]{:S(2)}) collective-permute-start(f32[3,8,1,256]{3,2,1,0:T(1,128)S(1)} %get-tuple-element.43), channel_id=1, source_target_pairs={{1,0},{2,1},{3,2},{4,3},{5,4},{6,5},{7,6},{8,7},{9,8},{10,9},{11,1... | collective-permute-start | bytes 73736 | tf_op jit(solution)/shard_map/ppermute | solution.py:168
  96.1 16.1 %collective-permute-start.1 = (f32[3,1,16,256]{3,2,1,0:T(8,128)S(1)}, f32[3,1,16,256]{3,2,1,0:T(8,128)S(1)}, u32[]{:S(2)}, u32[]{:S(2)}) collective-permute-start(f32[3,1,16,256]{3,2,1,0:T(8,128)S(1)} %get-tuple-element.54), channel_id=1, source_target_pairs={{0,16},{16,32},{32,48},{48,64},{64,80},{80,96},{96,112},{1,17},{17... | collective-permute-start | bytes 147464 | tf_op jit(solution)/shard_map/ppermute | solution.py:165
  98.0 14.3 %collective-permute-start = (f32[3,1,16,256]{3,2,1,0:T(8,128)S(1)}, f32[3,1,16,256]{3,2,1,0:T(8,128)S(1)}, u32[]{:S(2)}, u32[]{:S(2)}) collective-permute-start(f32[3,1,16,256]{3,2,1,0:T(8,128)S(1)} %get-tuple-element.53), channel_id=1, source_target_pairs={{16,0},{32,16},{48,32},{64,48},{80,64},{96,80},{112,96},{17,1},{33... | collective-permute-start | bytes 147464 | tf_op jit(solution)/shard_map/ppermute | solution.py:168
  104.2 14.0 %collective-permute-start.18 = (f32[3,8,1,256]{3,2,1,0:T(1,128)S(1)}, f32[3,8,1,256]{3,2,1,0:T(1,128)S(1)}, u32[]{:S(2)}, u32[]{:S(2)}) collective-permute-start(f32[3,8,1,256]{3,2,1,0:T(1,128)S(1)} %get-tuple-element.40), channel_id=1, source_target_pairs={{0,1},{1,2},{2,3},{3,4},{4,5},{5,6},{6,7},{7,8},{8,9},{9,10},{10,1... | collective-permute-start | bytes 73736 | tf_op jit(solution)/shard_map/ppermute | solution.py:165
  106.2 12.1 %collective-permute-start.19 = (f32[3,8,1,256]{3,2,1,0:T(1,128)S(1)}, f32[3,8,1,256]{3,2,1,0:T(1,128)S(1)}, u32[]{:S(2)}, u32[]{:S(2)}) collective-permute-start(f32[3,8,1,256]{3,2,1,0:T(1,128)S(1)} %get-tuple-element.41), channel_id=1, source_target_pairs={{1,0},{2,1},{3,2},{4,3},{5,4},{6,5},{7,6},{8,7},{9,8},{10,9},{11,1... | collective-permute-start | bytes 73736 | tf_op jit(solution)/shard_map/ppermute | solution.py:168
  112.4 6.9 %collective-permute-start.2 = (f32[3,10,1,256]{3,2,1,0:T(1,128)S(1)}, f32[3,10,1,256]{3,2,1,0:T(1,128)S(1)}, u32[]{:S(2)}, u32[]{:S(2)}) collective-permute-start(f32[3,10,1,256]{3,2,1,0:T(1,128)S(1)} %get-tuple-element.35), channel_id=1, source_target_pairs={{1,0},{2,1},{3,2},{4,3},{5,4},{6,5},{7,6},{8,7},{9,8},{10,9},{11,1... | collective-permute-start | bytes 92168 | tf_op jit(solution)/shard_map/ppermute | solution.py:168
  114.3 7.9 %collective-permute-start.3 = (f32[3,10,1,256]{3,2,1,0:T(1,128)S(1)}, f32[3,10,1,256]{3,2,1,0:T(1,128)S(1)}, u32[]{:S(2)}, u32[]{:S(2)}) collective-permute-start(f32[3,10,1,256]{3,2,1,0:T(1,128)S(1)} %get-tuple-element.34), channel_id=1, source_target_pairs={{0,1},{1,2},{2,3},{3,4},{4,5},{5,6},{6,7},{7,8},{8,9},{9,10},{10,1... | collective-permute-start | bytes 92168 | tf_op jit(solution)/shard_map/ppermute | solution.py:165
  119.3 3.5 %copy-start.10 = (f32[8,16,256]{2,1,0:T(8,128)S(1)}, f32[8,16,256]{2,1,0:T(8,128)}, u32[]{:S(2)}) copy-start(f32[8,16,256]{2,1,0:T(8,128)} %param.16) | copy-start | bytes 393220
  122.8 1.0 copy-start.12
  124.4 12.4 %collective-permute-start.4 = (f32[3,1,16,256]{3,2,1,0:T(8,128)S(1)}, f32[3,1,16,256]{3,2,1,0:T(8,128)S(1)}, u32[]{:S(2)}, u32[]{:S(2)}) collective-permute-start(f32[3,1,16,256]{3,2,1,0:T(8,128)S(1)} %get-tuple-element.49), channel_id=1, source_target_pairs={{16,0},{32,16},{48,32},{64,48},{80,64},{96,80},{112,96},{17,1},{33... | collective-permute-start | bytes 147464 | tf_op jit(solution)/shard_map/ppermute | solution.py:168
  126.3 10.4 %collective-permute-start.5 = (f32[3,1,16,256]{3,2,1,0:T(8,128)S(1)}, f32[3,1,16,256]{3,2,1,0:T(8,128)S(1)}, u32[]{:S(2)}, u32[]{:S(2)}) collective-permute-start(f32[3,1,16,256]{3,2,1,0:T(8,128)S(1)} %get-tuple-element.48), channel_id=1, source_target_pairs={{0,16},{16,32},{32,48},{48,64},{64,80},{80,96},{96,112},{1,17},{17... | collective-permute-start | bytes 147464 | tf_op jit(solution)/shard_map/ppermute | solution.py:165
  128.8 13.9 %collective-permute-start.20 = (f32[3,8,1,256]{3,2,1,0:T(1,128)S(1)}, f32[3,8,1,256]{3,2,1,0:T(1,128)S(1)}, u32[]{:S(2)}, u32[]{:S(2)}) collective-permute-start(f32[3,8,1,256]{3,2,1,0:T(1,128)S(1)} %get-tuple-element.38), channel_id=1, source_target_pairs={{0,1},{1,2},{2,3},{3,4},{4,5},{5,6},{6,7},{7,8},{8,9},{9,10},{10,1... | collective-permute-start | bytes 73736 | tf_op jit(solution)/shard_map/ppermute | solution.py:165
  130.7 12.0 %collective-permute-start.21 = (f32[3,8,1,256]{3,2,1,0:T(1,128)S(1)}, f32[3,8,1,256]{3,2,1,0:T(1,128)S(1)}, u32[]{:S(2)}, u32[]{:S(2)}) collective-permute-start(f32[3,8,1,256]{3,2,1,0:T(1,128)S(1)} %get-tuple-element.39), channel_id=1, source_target_pairs={{1,0},{2,1},{3,2},{4,3},{5,4},{6,5},{7,6},{8,7},{9,8},{10,9},{11,1... | collective-permute-start | bytes 73736 | tf_op jit(solution)/shard_map/ppermute | solution.py:168
  136.8 6.4 %collective-permute-start.6 = (f32[3,10,1,256]{3,2,1,0:T(1,128)S(1)}, f32[3,10,1,256]{3,2,1,0:T(1,128)S(1)}, u32[]{:S(2)}, u32[]{:S(2)}) collective-permute-start(f32[3,10,1,256]{3,2,1,0:T(1,128)S(1)} %get-tuple-element.33), channel_id=1, source_target_pairs={{1,0},{2,1},{3,2},{4,3},{5,4},{6,5},{7,6},{8,7},{9,8},{10,9},{11,1... | collective-permute-start | bytes 92168 | tf_op jit(solution)/shard_map/ppermute | solution.py:168
  138.8 7.9 %collective-permute-start.7 = (f32[3,10,1,256]{3,2,1,0:T(1,128)S(1)}, f32[3,10,1,256]{3,2,1,0:T(1,128)S(1)}, u32[]{:S(2)}, u32[]{:S(2)}) collective-permute-start(f32[3,10,1,256]{3,2,1,0:T(1,128)S(1)} %get-tuple-element.32), channel_id=1, source_target_pairs={{0,1},{1,2},{2,3},{3,4},{4,5},{5,6},{6,7},{7,8},{8,9},{9,10},{10,1... | collective-permute-start | bytes 92168 | tf_op jit(solution)/shard_map/ppermute | solution.py:165
  147.7 4.8 %collective-permute-start.8 = (f32[3,1,16,256]{3,2,1,0:T(8,128)S(1)}, f32[3,1,16,256]{3,2,1,0:T(8,128)S(1)}, u32[]{:S(2)}, u32[]{:S(2)}) collective-permute-start(f32[3,1,16,256]{3,2,1,0:T(8,128)S(1)} %get-tuple-element.47), channel_id=1, source_target_pairs={{16,0},{32,16},{48,32},{64,48},{80,64},{96,80},{112,96},{17,1},{33... | collective-permute-start | bytes 147464 | tf_op jit(solution)/shard_map/ppermute | solution.py:168
  149.7 5.4 %collective-permute-start.9 = (f32[3,1,16,256]{3,2,1,0:T(8,128)S(1)}, f32[3,1,16,256]{3,2,1,0:T(8,128)S(1)}, u32[]{:S(2)}, u32[]{:S(2)}) collective-permute-start(f32[3,1,16,256]{3,2,1,0:T(8,128)S(1)} %get-tuple-element.46), channel_id=1, source_target_pairs={{0,16},{16,32},{32,48},{48,64},{64,80},{80,96},{96,112},{1,17},{17... | collective-permute-start | bytes 147464 | tf_op jit(solution)/shard_map/ppermute | solution.py:165
  155.1 14.1 %collective-permute-start.10 = (f32[3,10,1,256]{3,2,1,0:T(1,128)S(1)}, f32[3,10,1,256]{3,2,1,0:T(1,128)S(1)}, u32[]{:S(2)}, u32[]{:S(2)}) collective-permute-start(f32[3,10,1,256]{3,2,1,0:T(1,128)S(1)} %get-tuple-element.31), channel_id=1, source_target_pairs={{1,0},{2,1},{3,2},{4,3},{5,4},{6,5},{7,6},{8,7},{9,8},{10,9},{11,1... | collective-permute-start | bytes 92168 | tf_op jit(solution)/shard_map/ppermute | solution.py:168
  157.0 12.1 %collective-permute-start.11 = (f32[3,10,1,256]{3,2,1,0:T(1,128)S(1)}, f32[3,10,1,256]{3,2,1,0:T(1,128)S(1)}, u32[]{:S(2)}, u32[]{:S(2)}) collective-permute-start(f32[3,10,1,256]{3,2,1,0:T(1,128)S(1)} %get-tuple-element.30), channel_id=1, source_target_pairs={{0,1},{1,2},{2,3},{3,4},{4,5},{5,6},{6,7},{7,8},{8,9},{9,10},{10,1... | collective-permute-start | bytes 92168 | tf_op jit(solution)/shard_map/ppermute | solution.py:165
  161.0 13.6 %collective-permute-start.22 = (f32[3,8,1,256]{3,2,1,0:T(1,128)S(1)}, f32[3,8,1,256]{3,2,1,0:T(1,128)S(1)}, u32[]{:S(2)}, u32[]{:S(2)}) collective-permute-start(f32[3,8,1,256]{3,2,1,0:T(1,128)S(1)} %get-tuple-element.36), channel_id=1, source_target_pairs={{0,1},{1,2},{2,3},{3,4},{4,5},{5,6},{6,7},{7,8},{8,9},{9,10},{10,1... | collective-permute-start | bytes 73736 | tf_op jit(solution)/shard_map/ppermute | solution.py:165
  163.0 11.7 %collective-permute-start.23 = (f32[3,8,1,256]{3,2,1,0:T(1,128)S(1)}, f32[3,8,1,256]{3,2,1,0:T(1,128)S(1)}, u32[]{:S(2)}, u32[]{:S(2)}) collective-permute-start(f32[3,8,1,256]{3,2,1,0:T(1,128)S(1)} %get-tuple-element.37), channel_id=1, source_target_pairs={{1,0},{2,1},{3,2},{4,3},{5,4},{6,5},{7,6},{8,7},{9,8},{10,9},{11,1... | collective-permute-start | bytes 73736 | tf_op jit(solution)/shard_map/ppermute | solution.py:168
  170.2 4.9 %collective-permute-start.12 = (f32[3,1,16,256]{3,2,1,0:T(8,128)S(1)}, f32[3,1,16,256]{3,2,1,0:T(8,128)S(1)}, u32[]{:S(2)}, u32[]{:S(2)}) collective-permute-start(f32[3,1,16,256]{3,2,1,0:T(8,128)S(1)} %get-tuple-element.45), channel_id=1, source_target_pairs={{16,0},{32,16},{48,32},{64,48},{80,64},{96,80},{112,96},{17,1},{33... | collective-permute-start | bytes 147464 | tf_op jit(solution)/shard_map/ppermute | solution.py:168
  172.2 5.4 %collective-permute-start.13 = (f32[3,1,16,256]{3,2,1,0:T(8,128)S(1)}, f32[3,1,16,256]{3,2,1,0:T(8,128)S(1)}, u32[]{:S(2)}, u32[]{:S(2)}) collective-permute-start(f32[3,1,16,256]{3,2,1,0:T(8,128)S(1)} %get-tuple-element.44), channel_id=1, source_target_pairs={{0,16},{16,32},{32,48},{48,64},{64,80},{80,96},{96,112},{1,17},{17... | collective-permute-start | bytes 147464 | tf_op jit(solution)/shard_map/ppermute | solution.py:165
  177.6 7.1 %collective-permute-start.14 = (f32[3,10,1,256]{3,2,1,0:T(1,128)S(1)}, f32[3,10,1,256]{3,2,1,0:T(1,128)S(1)}, u32[]{:S(2)}, u32[]{:S(2)}) collective-permute-start(f32[3,10,1,256]{3,2,1,0:T(1,128)S(1)} %get-tuple-element.29), channel_id=1, source_target_pairs={{1,0},{2,1},{3,2},{4,3},{5,4},{6,5},{7,6},{8,7},{9,8},{10,9},{11,1... | collective-permute-start | bytes 92168 | tf_op jit(solution)/shard_map/ppermute | solution.py:168
  179.6 7.9 %collective-permute-start.15 = (f32[3,10,1,256]{3,2,1,0:T(1,128)S(1)}, f32[3,10,1,256]{3,2,1,0:T(1,128)S(1)}, u32[]{:S(2)}, u32[]{:S(2)}) collective-permute-start(f32[3,10,1,256]{3,2,1,0:T(1,128)S(1)} %get-tuple-element.28), channel_id=1, source_target_pairs={{0,1},{1,2},{2,3},{3,4},{4,5},{5,6},{6,7},{7,8},{8,9},{9,10},{10,1... | collective-permute-start | bytes 92168 | tf_op jit(solution)/shard_map/ppermute | solution.py:165
  (5 other events, 4.6 us)

commit v2 on v0

v2 whole, which is shorter than its diff:
```python
import jax
import jax.numpy as jnp
from jax import lax
from jax.experimental import pallas as pl
from jax.experimental.pallas import tpu as pltpu
from jax.sharding import PartitionSpec as P

BF = jnp.bfloat16
F32 = jnp.float32
MESH = pl.DeviceIdType.MESH
SWEEPS = 4


def split(x):
    hi = x.astype(BF)
    lo = (x - hi.astype(F32)).astype(BF)
    return hi, lo


def place(device):
    return (device // 16, device % 16)


def iota(shape, dim):
    return lax.broadcasted_iota(jnp.int32, shape, dim)


def build_table(field, table):
    x = field[...].reshape(384, 256)
    hi, lo = split(x)
    table[0:384, :] = hi
    table[768:1152, :] = lo
    hi, lo = split(pltpu.roll(x, 255, 1))
    table[384:768, :] = hi
    table[1152:1536, :] = lo


def interpolate_tile(t, cells, weights, out, table):
    z_iota = iota((256, 128), 0).astype(F32).astype(BF)
    y_iota = iota((16, 128), 0)
    tile = cells[0, pl.ds(pl.multiple_of(t * 8, 8), 8), :]
    z_tile = (tile & 255).astype(F32).astype(BF)
    y_tile = (tile >> 8) & 15
    x_tile = tile >> 12
    for pair in range(4):
        hot = [
            jnp.where(z_iota == z_tile[s : s + 1, :], jnp.ones((), BF), jnp.zeros((), BF))
            for s in (2 * pair, 2 * pair + 1)
        ]
        hot = jnp.concatenate(hot, axis=1)
        got = jnp.dot(table[0:768, :], hot, preferred_element_type=F32)
        got = got + jnp.dot(table[768:1536, :], hot, preferred_element_type=F32)
        for half in range(2):
            s = 2 * pair + half
            r = t * 8 + s
            w = weights[0, r]
            y_row = y_tile[s : s + 1, :]
            x_row = jnp.broadcast_to(x_tile[s : s + 1, :], (16, 128))
            y_here = y_iota == y_row
            y_next = y_iota == y_row + 1
            by_y = {}
            for a in range(2):
                for zc in range(2):
                    k = 4 * a + zc
                    by_y[a, zc] = jnp.where(
                        y_here, w[k : k + 1, :], jnp.where(y_next, w[k + 2 : k + 3, :], 0.0)
                    )
            acc = [None] * 3
            before = None
            for xx in range(8):
                here = x_row == xx if xx < 7 else None
                for zc in range(2):
                    coef = None
                    if before is not None:
                        coef = jnp.where(before, by_y[1, zc], 0.0)
                    if here is not None:
                        coef = jnp.where(here, by_y[0, zc], 0.0 if coef is None else coef)
                    for c in range(3):
                        at = zc * 384 + c * 128 + xx * 16
                        term = coef * got[at : at + 16, half * 128 : half * 128 + 128]
                        acc[c] = term if acc[c] is None else acc[c] + term
                before = here
            for c in range(3):
                out[r, c, :] = jnp.sum(acc[c], axis=0)


def interpolate(field, cells, weights, sent, came, table, sems, me):
    build_table(field, table)
    mine = me // 8

    def send(target):
        pltpu.make_async_remote_copy(
            src_ref=sent.at[target],
            dst_ref=came.at[me],
            send_sem=sems.at[0],
            recv_sem=sems.at[1],
            device_id=place(target),
            device_id_type=MESH,
        ).start()

    def step(i, carry):
        t = (mine + 1 + i) % 16
        interpolate_tile(t, cells, weights, sent, table)

        @pl.when(i < 15)
        def _():
            for s in range(8):
                send(t * 8 + (me + s) % 8)

        return carry

    lax.fori_loop(0, 16, step, 0)
    for s in range(1, 8):
        send(mine * 8 + (me + s) % 8)
    came[me] = sent[me]


def all_of(sent, came, sems, me):
    return pltpu.make_async_remote_copy(
        src_ref=sent.at[pl.ds(0, 127)],
        dst_ref=came.at[pl.ds(0, 127)],
        send_sem=sems.at[0],
        recv_sem=sems.at[1],
        device_id=place((me + 1) % 128),
        device_id_type=MESH,
    )


def overwrite(field, receptors, got, start, frozen, left, total):
    z_iota = iota((256, 128), 0).astype(F32).astype(BF)
    r_iota = iota((128, 128), 0).astype(F32).astype(BF)
    one = jnp.ones((), BF)
    zero = jnp.zeros((), BF)
    total[...] = jnp.zeros_like(total)

    def step(i, carry):
        tile = receptors[0, pl.ds(pl.multiple_of(i * 8, 8), 8), :]
        z_tile = (tile & 255).astype(F32).astype(BF)
        r_tile = (tile >> 8).astype(F32).astype(BF)
        hots = []
        for s in range(8):
            hots.append(jnp.where(z_iota == z_tile[s : s + 1, :], one, zero))
            mine = r_iota == r_tile[s : s + 1, :]
            hi, lo = split(got[i * 8 + s])
            at = slice(s * 128, s * 128 + 128)
            for c in range(3):
                left[c * 128 : c * 128 + 128, at] = jnp.where(mine, hi[c : c + 1, :], zero)
                left[384 + c * 128 : 512 + c * 128, at] = jnp.where(mine, lo[c : c + 1, :], zero)
            left[768:896, at] = jnp.where(mine, one, zero)
        hot = jnp.concatenate(hots, axis=1)
        total[...] += lax.dot_general(
            left[...], hot, (((1,), (1,)), ((), ())), preferred_element_type=F32
        )
        return carry

    lax.fori_loop(0, 16, step, 0)
    mask = total[768:896, :]
    frozen[...] = mask.reshape(8, 16, 256)
    for c in range(3):
        value = total[c * 128 : c * 128 + 128, :] + total[384 + c * 128 : 512 + c * 128, :]
        old = field[c].reshape(128, 256)
        start[c, 1:9] = jnp.where(mask > 0.5, value, old).reshape(8, 16, 256)


def halo_copies(grid, k, velocity, edge, halo, send_sems, recv_sems, g, s):
    north, south = (s + 1) % 16, (s + 15) % 16
    plan = [
        (edge.at[grid, k, 0], halo.at[grid, k, 0], (g, north)),
        (edge.at[grid, k, 1], halo.at[grid, k, 1], (g, south)),
    ]
    if grid == 0:
        plan += [
            (velocity.at[k, :, 8], velocity.at[k, :, 0], ((g + 1) % 8, s)),
            (velocity.at[k, :, 1], velocity.at[k, :, 9], ((g + 7) % 8, s)),
        ]
    return [
        pltpu.make_async_remote_copy(
            src_ref=source,
            dst_ref=target,
            send_sem=send_sems.at[grid, k, n],
            recv_sem=recv_sems.at[grid, k, n],
            device_id=device,
            device_id_type=MESH,
        )
        for n, (source, target, device) in enumerate(plan)
    ]


def fill_edges(grid, k, velocity, edge):
    for c in range(3):
        edge[grid, k, 0, c] = velocity[k, c, 1:9, 15, :]
        edge[grid, k, 1, c] = velocity[k, c, 1:9, 0, :]


def shifted(plane, low, high):
    y = iota((16, 256), 0)
    after_y = jnp.where(y == 15, high, pltpu.roll(plane, 15, 0))
    before_y = jnp.where(y == 0, low, pltpu.roll(plane, 1, 0))
    return after_y, before_y, pltpu.roll(plane, 255, 1), pltpu.roll(plane, 1, 1)


def assemble(grid, velocity, halo, source, inertia, frozen, coef, rhs, g, s):
    y = iota((16, 256), 0)
    z = iota((16, 256), 1)
    y_low = jnp.where(s > 0, 1.0, 0.0)
    y_high = jnp.where(s < 15, 1.0, 0.0)

    def face(middle, other, sign):
        return 1.0 + jnp.maximum(sign * (middle + other), 0.0)

    def step(x, carry):
        u, v, w = (velocity[0, c, x + 1] for c in range(3))
        if grid == 0:
            x_low = jnp.where((x > 0) | (g > 0), 1.0, 0.0)
            x_high = jnp.where((x < 7) | (g < 7), 1.0, 0.0)
        else:
            x_low = jnp.where(x > 0, 1.0, 0.0)
            x_high = jnp.where(x < 7, 1.0, 0.0)
        low = halo[grid, 0, 0, 1, pl.ds(x, 1), :] * y_low
        high = halo[grid, 0, 1, 1, pl.ds(x, 1), :] * y_high
        v_after, v_before, _, _ = shifted(v, low, high)
        w_after = jnp.where(z == 255, 0.0, pltpu.roll(w, 255, 1))
        w_before = jnp.where(z == 0, 0.0, pltpu.roll(w, 1, 1))
        faces = [
            face(u, velocity[0, 0, x + 2] * x_high, -0.5),
            face(u, velocity[0, 0, x] * x_low, 0.5),
            face(v, v_after, -0.5),
            face(v, v_before, 0.5),
            face(w, w_after, -0.5),
            face(w, w_before, 0.5),
        ]
        weight = inertia[x]
        diagonal = weight
        for f in faces:
            diagonal = diagonal + f
        inverse = 1.0 / diagonal
        stuck = frozen[x] > 0.5
        live = jnp.where(stuck, 0.0, inverse)
        faces = [f * live for f in faces]
        coef[0, x] = faces[0] * x_high
        coef[1, x] = faces[1] * x_low
        coef[2, x] = jnp.where(y == 15, faces[2] * y_high, faces[2])
        coef[3, x] = jnp.where(y == 0, faces[3] * y_low, faces[3])
        coef[4, x] = jnp.where(z == 255, 0.0, faces[4])
        coef[5, x] = jnp.where(z == 0, 0.0, faces[5])
        for c, start in enumerate((u, v, w)):
            right = (source[c, x] + weight * start) * inverse
            rhs[c, x] = jnp.where(stuck, start, right)
        return carry

    lax.fori_loop(0, 8, step, 0)


def sweep(grid, k, velocity, halo, coef, rhs, write):
    def step(x, carry):
        for c in range(3):
            after_y, before_y, after_z, before_z = shifted(
                velocity[k, c, x + 1],
                halo[grid, k, 0, c, pl.ds(x, 1), :],
                halo[grid, k, 1, c, pl.ds(x, 1), :],
            )
            total = rhs[c, x]
            total = total + coef[0, x] * velocity[k, c, x + 2] + coef[1, x] * velocity[k, c, x]
            total = total + coef[2, x] * after_y + coef[3, x] * before_y
            total = total + coef[4, x] * after_z + coef[5, x] * before_z
            write(c, x, total)
        return carry

    lax.fori_loop(0, 8, step, 0)


def kernel(*refs):
    (
        bg_vel_hbm, nb_vel_hbm, bg_source_hbm, nb_source_hbm, bg_inertia_hbm, nb_inertia_hbm,
        bg_cells_hbm, bg_weights_hbm, nb_cells_hbm, nb_weights_hbm, nb_rec_hbm, bg_rec_hbm,
        bg_out, nb_out,
        bg_vel, nb_vel, bg_source, nb_source, bg_inertia, nb_inertia,
        bg_cells, bg_weights, nb_cells, nb_weights, nb_rec, bg_rec,
        table, left, total,
        bg_sent, nb_sent, to_near, to_back, bg_run, nb_run,
        bg_frozen, nb_frozen, bg_coef, nb_coef, bg_rhs, nb_rhs, edge, halo,
        load_sems, near_sems, back_sems, send_sems, recv_sems, store_sems,
    ) = refs
    g = lax.axis_index("grp")
    s = lax.axis_index("sub")
    me = g * 16 + s

    hbm = refs[:12]
    vmem = refs[14:26]
    loads = [
        pltpu.make_async_copy(hbm[n], vmem[n], load_sems.at[n]) for n in range(12)
    ]
    for n in (0, 6, 7, 1, 8, 9, 10, 11, 2, 3, 4, 5):
        loads[n].start()

    barrier = pltpu.get_barrier_semaphore()

    def greet(i, carry):
        pl.semaphore_signal(
            barrier, inc=1, device_id=place((me + i) % 128), device_id_type=MESH
        )
        return carry

    lax.fori_loop(1, 128, greet, 0)
    pl.semaphore_wait(barrier, 127)
    for k in range(SWEEPS):
        for c in range(3):
            nb_run[k, c, 0] = jnp.zeros((16, 256), F32)
            nb_run[k, c, 9] = jnp.zeros((16, 256), F32)

    for n in (0, 6, 7):
        loads[n].wait()
    interpolate(bg_vel, bg_cells, bg_weights, bg_sent, to_near, table, near_sems, me)
    for n in (1, 8, 9):
        loads[n].wait()
    interpolate(nb_vel, nb_cells, nb_weights, nb_sent, to_back, table, back_sems, me)
    for n in (10, 11, 2, 3, 4, 5):
        loads[n].wait()

    copies = []

    def exchange(grid, k, velocity):
        fill_edges(grid, k, velocity, edge)
        new = halo_copies(grid, k, velocity, edge, halo, send_sems, recv_sems, g, s)
        for copy in new:
            copy.start()
        copies.extend(new)
        return new

    near = all_of(bg_sent, to_near, near_sems, me)
    near.wait_recv()
    overwrite(nb_vel, nb_rec, to_near, nb_run.at[0], nb_frozen, left, total)
    nb_moving = exchange(1, 0, nb_run)
    back = all_of(nb_sent, to_back, back_sems, me)
    back.wait_recv()
    overwrite(bg_vel, bg_rec, to_back, bg_run.at[0], bg_frozen, left, total)
    bg_moving = exchange(0, 0, bg_run)

    for k in range(SWEEPS):
        for copy in nb_moving:
            copy.wait_recv()
        if k == 0:
            assemble(1, nb_run, halo, nb_source, nb_inertia, nb_frozen, nb_coef, nb_rhs, g, s)

        def nb_write(c, x, value):
            if k < SWEEPS - 1:
                nb_run[k + 1, c, x + 1] = value
            else:
                nb_out[c, x] = value

        sweep(1, k, nb_run, halo, nb_coef, nb_rhs, nb_write)
        if k < SWEEPS - 1:
            nb_moving = exchange(1, k + 1, nb_run)
        for copy in bg_moving:
            copy.wait_recv()
        if k == 0:
            assemble(0, bg_run, halo, bg_source, bg_inertia, bg_frozen, bg_coef, bg_rhs, g, s)

        def bg_write(c, x, value):
            if k < SWEEPS - 1:
                bg_run[k + 1, c, x + 1] = value
            else:
                bg_out[c, x] = value

        sweep(0, k, bg_run, halo, bg_coef, bg_rhs, bg_write)
        if k < SWEEPS - 1:
            bg_moving = exchange(0, k + 1, bg_run)

    near.wait_send()
    back.wait_send()
    for copy in copies:
        copy.wait_send()


def body(*args):
    out = jax.ShapeDtypeStruct((3, 8, 16, 256), F32)
    vmem = pltpu.VMEM
    return pl.pallas_call(
        kernel,
        out_shape=(out, out),
        in_specs=[pl.BlockSpec(memory_space=pl.ANY)] * 12,
        out_specs=[pl.BlockSpec(memory_space=vmem)] * 2,
        scratch_shapes=[vmem(a.shape, a.dtype) for a in args]
        + [
            vmem((1536, 256), BF),
            vmem((896, 1024), BF),
            vmem((896, 256), F32),
            vmem((128, 4, 128), F32),
            vmem((128, 4, 128), F32),
            vmem((128, 4, 128), F32),
            vmem((128, 4, 128), F32),
            vmem((SWEEPS, 3, 10, 16, 256), F32),
            vmem((SWEEPS, 3, 10, 16, 256), F32),
            vmem((8, 16, 256), F32),
            vmem((8, 16, 256), F32),
            vmem((6, 8, 16, 256), F32),
            vmem((6, 8, 16, 256), F32),
            vmem((3, 8, 16, 256), F32),
            vmem((3, 8, 16, 256), F32),
            vmem((2, SWEEPS, 2, 3, 8, 256), F32),
            vmem((2, SWEEPS, 2, 3, 8, 256), F32),
            pltpu.SemaphoreType.DMA((12,)),
            pltpu.SemaphoreType.DMA((2,)),
            pltpu.SemaphoreType.DMA((2,)),
            pltpu.SemaphoreType.DMA((2, SWEEPS, 4)),
            pltpu.SemaphoreType.DMA((2, SWEEPS, 4)),
            pltpu.SemaphoreType.DMA((2,)),
        ],
        compiler_params=pltpu.CompilerParams(
            collective_id=0, has_side_effects=True, vmem_limit_bytes=48 * 2**20
        ),
        name="overset",
    )(*args)


def solution(mesh):
    return jax.shard_map(
        body,
        mesh=mesh,
        in_specs=(
            P(None, "grp", "sub", None),
            P(None, "grp", "sub", None),
            P(None, "grp", "sub", None),
            P(None, "grp", "sub", None),
            P("grp", "sub", None),
            P("grp", "sub", None),
            P(("grp", "sub"), None, None),
            P(("grp", "sub"), None, None, None),
            P(("grp", "sub"), None, None),
            P(("grp", "sub"), None, None, None),
            P(("grp", "sub"), None, None),
            P(("grp", "sub"), None, None),
        ),
        out_specs=(P(None, "grp", "sub", None), P(None, "grp", "sub", None)),
        check_vma=False,
    )
```

time: 1390 us -> 112 us (0.08)
  local copies, waits for them, and re-layouts: 1220 us -> 12.7 us
  Pallas kernels: 0 us -> 97.6 us
  starting transfers between devices: 91 us -> 0 us
  other arithmetic: 62.3 us -> 0 us
    gather x2 -> x0, local copies, waits for them, and re-layouts: 874 us -> none  [interpolate(): values = flat_field[:, indices]]
    scatter x4 -> x0, local copies, waits for them, and re-layouts: 225 us -> none  [the longest x2 121 us: overwrite(): jnp.zeros((1, cells_total), jnp.float32).at[:, indices]]
    pallas_call x0 -> x1, Pallas kernels: none -> 97.6 us  [body(): pl.pallas_call(kernel, out_shape=(out, out), in_specs=[pl.BlockSpec(memor...]
    ppermute x24 -> x0, starting transfers between devices: 70.1 us -> none  [the longest x12 54.4 us: extended(): lax.ppermute(lax.slice_in_dim(block, block.shape[dim] - width, None, axis...]
    slice x11 -> x0, local copies, waits for them, and re-layouts: 61.1 us -> none  [the longest x3 60.9 us: assemble(): middle[direction] + after_cells[direction][direction]]
    reduce_sum x2 -> x0, other arithmetic: 50.9 us -> none  [interpolate(): return jnp.sum(values * weights[None], axis=2)]
    reshape x4 -> x0, local copies, waits for them, and re-layouts: 30.2 us -> none  [the longest x2 10.2 us: overwrite(): values.reshape(values.shape[0], -1)]
    all_to_all x2 -> x0, starting transfers between devices: 20.9 us -> none  [the longest x1 11.1 us: body(): lax.all_to_all(to_near, ('grp', 'sub'), split_axis=1, concat_axis=1, tile...]
  transfers between devices with their start and end apart: 26 -> 0, of which waited for: 5 -> 0; matrix products, arithmetic and copies ran while one was open for 58% -> 0% of each run, Pallas kernels for 0% -> 0%
where the time goes in v2:
time: 112 us; the launch traced here: 111 us
  Pallas kernels  97.6 us (87%)
  local copies, waits for them, and re-layouts  12.7 us (11%)
    pallas_call x1, Pallas kernels, body(): pl.pallas_call(kernel, out_shape=(out, out), in_specs=[pl.BlockSpec(memor...  97.6 us
    unnamed x26, local copies, waits for them, and re-layouts  12.7 us

profile of v2, /device:TPU:0, one launch (start us, length us, event | category | flops | bytes accessed | tf_op | source)
XLA Modules:
  0.0 110.9 jit_solution(5334934680592201114)
XLA Ops:
  0.6 0.0 copy-start
  0.6 1.0 copy-done
  1.7 0.0 copy-start.1
  1.7 1.0 copy-done.1
  2.7 0.0 copy-start.2
  2.7 1.0 copy-done.2
  3.7 0.0 copy-start.3
  3.7 1.0 copy-done.3
  4.7 0.0 copy-start.4
  4.7 1.0 copy-done.4
  5.7 0.0 copy-start.5
  5.7 1.0 copy-done.5
  6.7 0.0 copy-start.6
  6.7 0.9 copy-done.6
  7.6 0.0 copy-start.7
  7.6 0.9 copy-done.7
  8.5 0.0 copy-start.8
  8.5 0.8 copy-done.8
  9.4 0.0 copy-start.9
  9.4 0.8 copy-done.9
  10.2 0.0 copy-start.10
  10.2 0.8 copy-done.10
  11.0 0.0 copy-start.11
  11.0 0.8 copy-done.11
  11.9 97.6 %overset.1 = (f32[3,8,16,256]{3,2,1,0:T(8,128)S(1)}, f32[3,8,16,256]{3,2,1,0:T(8,128)S(1)}) custom-call(f32[3,8,16,256]{3,2,1,0:T(8,128)S(1)} %copy-done.2, f32[3,8,16,256]{3,2,1,0:T(8,128)S(1)} %copy-done.3, f32[3,8,16,256]{3,2,1,0:T(8,128)S(1)} %copy-done.4, f32[3,8,16,256]{3,2,1,0:T(8,128)S(1)} %copy-done.5, f32[8,16,256]{2,1,0:T(8,128)S(1)} %copy-done.6, ...), custom_call_target="tpu_custom_call" | custom-call | tf_op jit(solution)/shard_map/overset/pallas_call | solution.py:378
  109.4 0.7 copy.16
  110.2 0.7 copy.17
Async XLA Ops:
  0.6 1.0 copy-start
  1.7 1.0 copy-start.1
  2.7 1.0 copy-start.2
  3.7 1.0 copy-start.3
  4.7 1.0 copy-start.4
  5.7 1.0 copy-start.5
  6.7 0.9 copy-start.6
  7.6 0.9 copy-start.7
  8.5 0.8 copy-start.8
  9.4 0.8 copy-start.9
  10.2 0.8 copy-start.10
  11.0 0.8 copy-start.11

commit v3 on v2

--- a/solution.py
+++ b/solution.py
@@ -26,13 +26,14 @@
 
 
 def build_table(field, table):
-    x = field[...].reshape(384, 256)
-    hi, lo = split(x)
-    table[0:384, :] = hi
-    table[768:1152, :] = lo
-    hi, lo = split(pltpu.roll(x, 255, 1))
-    table[384:768, :] = hi
-    table[1152:1536, :] = lo
+    for c in range(3):
+        here = field[c].reshape(128, 256)
+        for zc, x in enumerate((here, pltpu.roll(here, 255, 1))):
+            hi, lo = split(x)
+            for xx in range(8):
+                at = xx * 96 + zc * 48 + c * 16
+                table[at : at + 16, :] = hi[xx * 16 : xx * 16 + 16]
+                table[768 + at : 784 + at, :] = lo[xx * 16 : xx * 16 + 16]
 
 
 def interpolate_tile(t, cells, weights, out, table):
@@ -76,7 +77,7 @@
                     if here is not None:
                         coef = jnp.where(here, by_y[0, zc], 0.0 if coef is None else coef)
                     for c in range(3):
-                        at = zc * 384 + c * 128 + xx * 16
+                        at = xx * 96 + zc * 48 + c * 16
                         term = coef * got[at : at + 16, half * 128 : half * 128 + 128]
                         acc[c] = term if acc[c] is None else acc[c] + term
                 before = here
@@ -84,11 +85,20 @@
                 out[r, c, :] = jnp.sum(acc[c], axis=0)
 
 
-def interpolate(field, cells, weights, sent, came, table, sems, me):
+def interpolate(field, cells, weights, sent, table, beside):
     build_table(field, table)
-    mine = me // 8
-
-    def send(target):
+
+    def step(i, carry):
+        beside(i)
+        interpolate_tile(i, cells, weights, sent, table)
+        return carry
+
+    lax.fori_loop(0, 16, step, 0)
+
+
+def sender(sent, came, sems, me):
+    def send(offset):
+        target = (me + offset) % 128
         pltpu.make_async_remote_copy(
             src_ref=sent.at[target],
             dst_ref=came.at[me],
@@ -98,21 +108,16 @@
             device_id_type=MESH,
         ).start()
 
-    def step(i, carry):
-        t = (mine + 1 + i) % 16
-        interpolate_tile(t, cells, weights, sent, table)
-
-        @pl.when(i < 15)
-        def _():
-            for s in range(8):
-                send(t * 8 + (me + s) % 8)
-
-        return carry
-
-    lax.fori_loop(0, 16, step, 0)
-    for s in range(1, 8):
-        send(mine * 8 + (me + s) % 8)
-    came[me] = sent[me]
+    def first():
+        for offset in range(1, 16):
+            send(offset)
+        came[me] = sent[me]
+
+    def some(i):
+        for n in range(7):
+            send(16 + 7 * i + n)
+
+    return first, some
 
 
 def all_of(sent, came, sems, me):
@@ -126,40 +131,45 @@
     )
 
 
-def overwrite(field, receptors, got, start, frozen, left, total):
+def overwrite(field, receptors, got, start, frozen, total, beside):
     z_iota = iota((256, 128), 0).astype(F32).astype(BF)
     r_iota = iota((128, 128), 0).astype(F32).astype(BF)
+    lift = jnp.where(iota((4, 128), 0) == 0, 8.0, 0.0)
     one = jnp.ones((), BF)
     zero = jnp.zeros((), BF)
     total[...] = jnp.zeros_like(total)
 
     def step(i, carry):
+        beside(i)
         tile = receptors[0, pl.ds(pl.multiple_of(i * 8, 8), 8), :]
         z_tile = (tile & 255).astype(F32).astype(BF)
         r_tile = (tile >> 8).astype(F32).astype(BF)
-        hots = []
-        for s in range(8):
-            hots.append(jnp.where(z_iota == z_tile[s : s + 1, :], one, zero))
-            mine = r_iota == r_tile[s : s + 1, :]
-            hi, lo = split(got[i * 8 + s])
-            at = slice(s * 128, s * 128 + 128)
-            for c in range(3):
-                left[c * 128 : c * 128 + 128, at] = jnp.where(mine, hi[c : c + 1, :], zero)
-                left[384 + c * 128 : 512 + c * 128, at] = jnp.where(mine, lo[c : c + 1, :], zero)
-            left[768:896, at] = jnp.where(mine, one, zero)
-        hot = jnp.concatenate(hots, axis=1)
-        total[...] += lax.dot_general(
-            left[...], hot, (((1,), (1,)), ((), ())), preferred_element_type=F32
-        )
+        for half in range(2):
+            hots = []
+            lefts = []
+            for s in range(4 * half, 4 * half + 4):
+                hots.append(jnp.where(z_iota == z_tile[s : s + 1, :], one, zero))
+                mine = r_iota == r_tile[s : s + 1, :]
+                parts = split(got[i * 8 + s] + lift)
+                rows = [jnp.where(mine, p[c : c + 1, :], zero) for p in parts for c in range(3)]
+                lefts.append(jnp.concatenate(rows, axis=0))
+            total[...] += lax.dot_general(
+                jnp.concatenate(lefts, axis=1),
+                jnp.concatenate(hots, axis=1),
+                (((1,), (1,)), ((), ())),
+                preferred_element_type=F32,
+            )
         return carry
 
     lax.fori_loop(0, 16, step, 0)
-    mask = total[768:896, :]
+    mask = total[0:128, :]
     frozen[...] = mask.reshape(8, 16, 256)
     for c in range(3):
         value = total[c * 128 : c * 128 + 128, :] + total[384 + c * 128 : 512 + c * 128, :]
+        if c == 0:
+            value = value - 8.0
         old = field[c].reshape(128, 256)
-        start[c, 1:9] = jnp.where(mask > 0.5, value, old).reshape(8, 16, 256)
+        start[c, 1:9] = jnp.where(mask > 1.0, value, old).reshape(8, 16, 256)
 
 
 def halo_copies(grid, k, velocity, edge, halo, send_sems, recv_sems, g, s):
@@ -199,7 +209,7 @@
     return after_y, before_y, pltpu.roll(plane, 255, 1), pltpu.roll(plane, 1, 1)
 
 
-def assemble(grid, velocity, halo, source, inertia, frozen, coef, rhs, g, s):
+def assemble(grid, velocity, halo, source, inertia, frozen, coef, rhs, rim, g, s):
     y = iota((16, 256), 0)
     z = iota((16, 256), 1)
     y_low = jnp.where(s > 0, 1.0, 0.0)
@@ -234,13 +244,13 @@
         for f in faces:
             diagonal = diagonal + f
         inverse = 1.0 / diagonal
-        stuck = frozen[x] > 0.5
+        stuck = frozen[x] > 1.0
         live = jnp.where(stuck, 0.0, inverse)
         faces = [f * live for f in faces]
         coef[0, x] = faces[0] * x_high
         coef[1, x] = faces[1] * x_low
-        coef[2, x] = jnp.where(y == 15, faces[2] * y_high, faces[2])
-        coef[3, x] = jnp.where(y == 0, faces[3] * y_low, faces[3])
+        coef[2, x] = faces[2]
+        coef[3, x] = faces[3]
         coef[4, x] = jnp.where(z == 255, 0.0, faces[4])
         coef[5, x] = jnp.where(z == 0, 0.0, faces[5])
         for c, start in enumerate((u, v, w)):
@@ -249,24 +259,40 @@
         return carry
 
     lax.fori_loop(0, 8, step, 0)
-
-
-def sweep(grid, k, velocity, halo, coef, rhs, write):
-    def step(x, carry):
+    rim[grid, 0] = coef[3, :, 0, :] * y_low
+    rim[grid, 1] = coef[2, :, 15, :] * y_high
+    coef[3, :, 0, :] = jnp.zeros((8, 256), F32)
+    coef[2, :, 15, :] = jnp.zeros((8, 256), F32)
+
+
+def inner(now, coef, rhs, after):
+    for x in range(8):
         for c in range(3):
-            after_y, before_y, after_z, before_z = shifted(
-                velocity[k, c, x + 1],
-                halo[grid, k, 0, c, pl.ds(x, 1), :],
-                halo[grid, k, 1, c, pl.ds(x, 1), :],
-            )
+            plane = now[c, x + 1]
             total = rhs[c, x]
-            total = total + coef[0, x] * velocity[k, c, x + 2] + coef[1, x] * velocity[k, c, x]
-            total = total + coef[2, x] * after_y + coef[3, x] * before_y
-            total = total + coef[4, x] * after_z + coef[5, x] * before_z
-            write(c, x, total)
-        return carry
-
-    lax.fori_loop(0, 8, step, 0)
+            if x < 7:
+                total = total + coef[0, x] * now[c, x + 2]
+            if x > 0:
+                total = total + coef[1, x] * now[c, x]
+            total = total + coef[2, x] * pltpu.roll(plane, 15, 0)
+            total = total + coef[3, x] * pltpu.roll(plane, 1, 0)
+            total = total + coef[4, x] * pltpu.roll(plane, 255, 1)
+            total = total + coef[5, x] * pltpu.roll(plane, 1, 1)
+            after[c, x] = total
+
+
+def outer(grid, k, now, halo, coef, rim, after, edge):
+    for c in range(3):
+        if grid == 0:
+            after[c, 0] = after[c, 0] + coef[1, 0] * now[c, 0]
+            after[c, 7] = after[c, 7] + coef[0, 7] * now[c, 9]
+        low = after[c, :, 0, :] + rim[grid, 0] * halo[grid, k, 0, c]
+        high = after[c, :, 15, :] + rim[grid, 1] * halo[grid, k, 1, c]
+        after[c, :, 0, :] = low
+        after[c, :, 15, :] = high
+        if k < SWEEPS - 1:
+            edge[grid, k + 1, 0, c] = high
+            edge[grid, k + 1, 1, c] = low
 
 
 def kernel(*refs):
@@ -276,10 +302,10 @@
         bg_out, nb_out,
         bg_vel, nb_vel, bg_source, nb_source, bg_inertia, nb_inertia,
         bg_cells, bg_weights, nb_cells, nb_weights, nb_rec, bg_rec,
-        table, left, total,
+        table, total,
         bg_sent, nb_sent, to_near, to_back, bg_run, nb_run,
-        bg_frozen, nb_frozen, bg_coef, nb_coef, bg_rhs, nb_rhs, edge, halo,
-        load_sems, near_sems, back_sems, send_sems, recv_sems, store_sems,
+        bg_frozen, nb_frozen, bg_coef, nb_coef, bg_rhs, nb_rhs, edge, halo, rim,
+        load_sems, near_sems, back_sems, send_sems, recv_sems,
     ) = refs
     g = lax.axis_index("grp")
     s = lax.axis_index("sub")
@@ -302,69 +328,65 @@
         return carry
 
     lax.fori_loop(1, 128, greet, 0)
-    pl.semaphore_wait(barrier, 127)
-    for k in range(SWEEPS):
-        for c in range(3):
-            nb_run[k, c, 0] = jnp.zeros((16, 256), F32)
-            nb_run[k, c, 9] = jnp.zeros((16, 256), F32)
-
+    for c in range(3):
+        nb_run[0, c, 0] = jnp.zeros((16, 256), F32)
+        nb_run[0, c, 9] = jnp.zeros((16, 256), F32)
+
+    near_first, near_some = sender(bg_sent, to_near, near_sems, me)
+    back_first, back_some = sender(nb_sent, to_back, back_sems, me)
     for n in (0, 6, 7):
         loads[n].wait()
-    interpolate(bg_vel, bg_cells, bg_weights, bg_sent, to_near, table, near_sems, me)
+    interpolate(bg_vel, bg_cells, bg_weights, bg_sent, table, lambda i: None)
     for n in (1, 8, 9):
         loads[n].wait()
-    interpolate(nb_vel, nb_cells, nb_weights, nb_sent, to_back, table, back_sems, me)
+    pl.semaphore_wait(barrier, 127)
+    near_first()
+    interpolate(nb_vel, nb_cells, nb_weights, nb_sent, table, near_some)
     for n in (10, 11, 2, 3, 4, 5):
         loads[n].wait()
+    back_first()
+    near = all_of(bg_sent, to_near, near_sems, me)
+    near.wait_recv()
+    overwrite(nb_vel, nb_rec, to_near, nb_run.at[0], nb_frozen, total, back_some)
 
     copies = []
 
     def exchange(grid, k, velocity):
-        fill_edges(grid, k, velocity, edge)
         new = halo_copies(grid, k, velocity, edge, halo, send_sems, recv_sems, g, s)
         for copy in new:
             copy.start()
         copies.extend(new)
         return new
 
-    near = all_of(bg_sent, to_near, near_sems, me)
-    near.wait_recv()
-    overwrite(nb_vel, nb_rec, to_near, nb_run.at[0], nb_frozen, left, total)
+    fill_edges(1, 0, nb_run, edge)
     nb_moving = exchange(1, 0, nb_run)
     back = all_of(nb_sent, to_back, back_sems, me)
     back.wait_recv()
-    overwrite(bg_vel, bg_rec, to_back, bg_run.at[0], bg_frozen, left, total)
-    bg_moving = exchange(0, 0, bg_run)
-
+    overwrite(bg_vel, bg_rec, to_back, bg_run.at[0], bg_frozen, total, lambda i: None)
+    fill_edges(0, 0, bg_run, edge)
+    moving = [exchange(0, 0, bg_run), nb_moving]
+
+    runs = (bg_run, nb_run)
+    outs = (bg_out, nb_out)
+    coefs = (bg_coef, nb_coef)
+    sides = (bg_rhs, nb_rhs)
+    fields = ((bg_source, bg_inertia, bg_frozen), (nb_source, nb_inertia, nb_frozen))
     for k in range(SWEEPS):
-        for copy in nb_moving:
-            copy.wait_recv()
-        if k == 0:
-            assemble(1, nb_run, halo, nb_source, nb_inertia, nb_frozen, nb_coef, nb_rhs, g, s)
-
-        def nb_write(c, x, value):
+        for grid in (1, 0):
+            run, coef, rhs = runs[grid], coefs[grid], sides[grid]
+            now = run.at[k]
+            after = run.at[k + 1, :, pl.ds(1, 8)] if k < SWEEPS - 1 else outs[grid]
+            if k == 0:
+                for copy in moving[grid]:
+                    copy.wait_recv()
+                assemble(grid, run, halo, *fields[grid], coef, rhs, rim, g, s)
+            inner(now, coef, rhs, after)
+            if k > 0:
+                for copy in moving[grid]:
+                    copy.wait_recv()
+            outer(grid, k, now, halo, coef, rim, after, edge)
             if k < SWEEPS - 1:
-                nb_run[k + 1, c, x + 1] = value
-            else:
-                nb_out[c, x] = value
-
-        sweep(1, k, nb_run, halo, nb_coef, nb_rhs, nb_write)
-        if k < SWEEPS - 1:
-            nb_moving = exchange(1, k + 1, nb_run)
-        for copy in bg_moving:
-            copy.wait_recv()
-        if k == 0:
-            assemble(0, bg_run, halo, bg_source, bg_inertia, bg_frozen, bg_coef, bg_rhs, g, s)
-
-        def bg_write(c, x, value):
-            if k < SWEEPS - 1:
-                bg_run[k + 1, c, x + 1] = value
-            else:
-                bg_out[c, x] = value
-
-        sweep(0, k, bg_run, halo, bg_coef, bg_rhs, bg_write)
-        if k < SWEEPS - 1:
-            bg_moving = exchange(0, k + 1, bg_run)
+                moving[grid] = exchange(grid, k + 1, run)
 
     near.wait_send()
     back.wait_send()
@@ -383,8 +405,7 @@
         scratch_shapes=[vmem(a.shape, a.dtype) for a in args]
         + [
             vmem((1536, 256), BF),
-            vmem((896, 1024), BF),
-            vmem((896, 256), F32),
+            vmem((768, 256), F32),
             vmem((128, 4, 128), F32),
             vmem((128, 4, 128), F32),
             vmem((128, 4, 128), F32),
@@ -399,15 +420,15 @@
             vmem((3, 8, 16, 256), F32),
             vmem((2, SWEEPS, 2, 3, 8, 256), F32),
             vmem((2, SWEEPS, 2, 3, 8, 256), F32),
+            vmem((2, 2, 8, 256), F32),
             pltpu.SemaphoreType.DMA((12,)),
             pltpu.SemaphoreType.DMA((2,)),
             pltpu.SemaphoreType.DMA((2,)),
             pltpu.SemaphoreType.DMA((2, SWEEPS, 4)),
             pltpu.SemaphoreType.DMA((2, SWEEPS, 4)),
-            pltpu.SemaphoreType.DMA((2,)),
         ],
         compiler_params=pltpu.CompilerParams(
-            collective_id=0, has_side_effects=True, vmem_limit_bytes=48 * 2**20
+            collective_id=0, has_side_effects=True, vmem_limit_bytes=63 * 2**20
         ),
         name="overset",
     )(*args)

time: 112 us -> 92.6 us (0.83)
  local copies, waits for them, and re-layouts: 12.7 us -> 2.57 us
  Pallas kernels: 97.6 us -> 89 us
    unnamed x26 -> x4, local copies, waits for them, and re-layouts: 12.7 us -> 2.57 us
    pallas_call x1, Pallas kernels: 97.6 us -> 89 us  [body(): pl.pallas_call(kernel, out_shape=(out, out), in_specs=[pl.BlockSpec(memor...]
where the time goes in v3:
time: 92.6 us; the launch traced here: 92.2 us
  Pallas kernels  89 us (96%)
  local copies, waits for them, and re-layouts  2.57 us (3%)
    pallas_call x1, Pallas kernels, body(): pl.pallas_call(kernel, out_shape=(out, out), in_specs=[pl.BlockSpec(memor...  89 us
    unnamed x4, local copies, waits for them, and re-layouts  2.57 us

profile of v3, /device:TPU:0, one launch (start us, length us, event | category | flops | bytes accessed | tf_op | source)
XLA Modules:
  0.0 92.2 jit_solution(9054673019378498268)
XLA Ops:
  0.6 89.0 %overset.1 = (f32[3,8,16,256]{3,2,1,0:T(8,128)}, f32[3,8,16,256]{3,2,1,0:T(8,128)}) custom-call(f32[3,8,16,256]{3,2,1,0:T(8,128)} %refs_0_.1, f32[3,8,16,256]{3,2,1,0:T(8,128)} %refs_1_.1, f32[3,8,16,256]{3,2,1,0:T(8,128)} %refs_2_.1, f32[3,8,16,256]{3,2,1,0:T(8,128)} %refs_3_.1, f32[8,16,256]{2,1,0:T(8,128)} %refs_4_.1, f32[8,16,256]{2,1,0:T(8,128)} %refs_5_.1, ...), custom_call_target="tpu_custom_call" | custom-call | tf_op jit(solution)/shard_map/overset/pallas_call | solution.py:400
  89.7 0.0 copy-start
  89.7 1.8 %copy.16 = f32[3,8,16,256]{3,2,1,0:T(8,128)} copy(f32[3,8,16,256]{3,2,1,0:T(8,128)} %get-tuple-element.4) | data formatting | bytes 786432
  91.5 0.0 copy-done
  91.5 0.7 copy.17
Async XLA Ops:
  89.7 1.8 %copy-start = (f32[3,8,16,256]{3,2,1,0:T(8,128)S(1)}, f32[3,8,16,256]{3,2,1,0:T(8,128)}, u32[]{:S(2)}) copy-start(f32[3,8,16,256]{3,2,1,0:T(8,128)} %get-tuple-element.5) | copy-start | bytes 1179652

commit v4 on v3

--- a/solution.py
+++ b/solution.py
@@ -9,16 +9,13 @@
 F32 = jnp.float32
 MESH = pl.DeviceIdType.MESH
 SWEEPS = 4
+HOP_STEP = 7
 
 
 def split(x):
     hi = x.astype(BF)
     lo = (x - hi.astype(F32)).astype(BF)
     return hi, lo
-
-
-def place(device):
-    return (device // 16, device % 16)
 
 
 def iota(shape, dim):
@@ -53,8 +50,7 @@
         got = got + jnp.dot(table[768:1536, :], hot, preferred_element_type=F32)
         for half in range(2):
             s = 2 * pair + half
-            r = t * 8 + s
-            w = weights[0, r]
+            w = weights[0, t * 8 + s]
             y_row = y_tile[s : s + 1, :]
             x_row = jnp.broadcast_to(x_tile[s : s + 1, :], (16, 128))
             y_here = y_iota == y_row
@@ -82,7 +78,7 @@
                         acc[c] = term if acc[c] is None else acc[c] + term
                 before = here
             for c in range(3):
-                out[r, c, :] = jnp.sum(acc[c], axis=0)
+                out[t // 2, (t % 2) * 8 + s, c, :] = jnp.sum(acc[c], axis=0)
 
 
 def interpolate(field, cells, weights, sent, table, beside):
@@ -96,39 +92,71 @@
     lax.fori_loop(0, 16, step, 0)
 
 
-def sender(sent, came, sems, me):
-    def send(offset):
-        target = (me + offset) % 128
-        pltpu.make_async_remote_copy(
-            src_ref=sent.at[target],
-            dst_ref=came.at[me],
-            send_sem=sems.at[0],
-            recv_sem=sems.at[1],
-            device_id=place(target),
+class Exchange:
+    def __init__(self, sent, held, came, sems, g, s):
+        self.sent, self.held, self.came, self.sems, self.g, self.s = sent, held, came, sems, g, s
+
+    def across(self, offset):
+        peer = (self.g + offset) % 8
+        return pltpu.make_async_remote_copy(
+            src_ref=self.sent.at[peer],
+            dst_ref=self.held.at[self.g],
+            send_sem=self.sems.at[0],
+            recv_sem=self.sems.at[1],
+            device_id=(peer, self.s),
             device_id_type=MESH,
-        ).start()
-
-    def first():
-        for offset in range(1, 16):
-            send(offset)
-        came[me] = sent[me]
-
-    def some(i):
-        for n in range(7):
-            send(16 + 7 * i + n)
-
-    return first, some
-
-
-def all_of(sent, came, sems, me):
-    return pltpu.make_async_remote_copy(
-        src_ref=sent.at[pl.ds(0, 127)],
-        dst_ref=came.at[pl.ds(0, 127)],
-        send_sem=sems.at[0],
-        recv_sem=sems.at[1],
-        device_id=place((me + 1) % 128),
-        device_id_type=MESH,
-    )
+        )
+
+    def along(self, offset):
+        peer = (self.s + offset) % 16
+        return pltpu.make_async_remote_copy(
+            src_ref=self.held.at[:, peer],
+            dst_ref=self.came.at[self.s],
+            send_sem=self.sems.at[2],
+            recv_sem=self.sems.at[3],
+            device_id=(self.g, peer),
+            device_id_type=MESH,
+        )
+
+    def all_across(self):
+        return pltpu.make_async_remote_copy(
+            src_ref=self.sent.at[pl.ds(0, 7)],
+            dst_ref=self.held.at[pl.ds(0, 7)],
+            send_sem=self.sems.at[0],
+            recv_sem=self.sems.at[1],
+            device_id=((self.g + 1) % 8, self.s),
+            device_id_type=MESH,
+        )
+
+    def all_along(self):
+        return pltpu.make_async_remote_copy(
+            src_ref=self.came.at[pl.ds(0, 15)],
+            dst_ref=self.came.at[pl.ds(0, 15)],
+            send_sem=self.sems.at[2],
+            recv_sem=self.sems.at[3],
+            device_id=(self.g, (self.s + 1) % 16),
+            device_id_type=MESH,
+        )
+
+    def first_hop(self):
+        for offset in (4, 3, 5, 2, 6, 1, 7):
+            self.across(offset).start()
+        self.held[self.g] = self.sent[self.g]
+
+    def second_hop(self, i):
+        @pl.when(i == HOP_STEP)
+        def _():
+            self.all_across().wait_recv()
+            for offset in range(1, 16):
+                self.along(offset).start()
+            self.came[self.s] = self.held[:, self.s]
+
+    def arrive(self):
+        self.all_along().wait_recv()
+
+    def finish(self):
+        self.all_across().wait_send()
+        self.all_along().wait_send()
 
 
 def overwrite(field, receptors, got, start, frozen, total, beside):
@@ -150,7 +178,7 @@
             for s in range(4 * half, 4 * half + 4):
                 hots.append(jnp.where(z_iota == z_tile[s : s + 1, :], one, zero))
                 mine = r_iota == r_tile[s : s + 1, :]
-                parts = split(got[i * 8 + s] + lift)
+                parts = split(got[(i % 2) * 8 + s, i // 2] + lift)
                 rows = [jnp.where(mine, p[c : c + 1, :], zero) for p in parts for c in range(3)]
                 lefts.append(jnp.concatenate(rows, axis=0))
             total[...] += lax.dot_general(
@@ -303,13 +331,12 @@
         bg_vel, nb_vel, bg_source, nb_source, bg_inertia, nb_inertia,
         bg_cells, bg_weights, nb_cells, nb_weights, nb_rec, bg_rec,
         table, total,
-        bg_sent, nb_sent, to_near, to_back, bg_run, nb_run,
+        bg_sent, nb_sent, bg_held, nb_held, to_near, to_back, bg_run, nb_run,
         bg_frozen, nb_frozen, bg_coef, nb_coef, bg_rhs, nb_rhs, edge, halo, rim,
         load_sems, near_sems, back_sems, send_sems, recv_sems,
     ) = refs
     g = lax.axis_index("grp")
     s = lax.axis_index("sub")
-    me = g * 16 + s
 
     hbm = refs[:12]
     vmem = refs[14:26]
@@ -321,33 +348,33 @@
 
     barrier = pltpu.get_barrier_semaphore()
 
-    def greet(i, carry):
+    for offset in range(1, 8):
         pl.semaphore_signal(
-            barrier, inc=1, device_id=place((me + i) % 128), device_id_type=MESH
-        )
-        return carry
-
-    lax.fori_loop(1, 128, greet, 0)
+            barrier, inc=1, device_id=((g + offset) % 8, s), device_id_type=MESH
+        )
+    for offset in range(1, 16):
+        pl.semaphore_signal(
+            barrier, inc=1, device_id=(g, (s + offset) % 16), device_id_type=MESH
+        )
     for c in range(3):
         nb_run[0, c, 0] = jnp.zeros((16, 256), F32)
         nb_run[0, c, 9] = jnp.zeros((16, 256), F32)
 
-    near_first, near_some = sender(bg_sent, to_near, near_sems, me)
-    back_first, back_some = sender(nb_sent, to_back, back_sems, me)
+    near = Exchange(bg_sent, bg_held, to_near, near_sems, g, s)
+    back = Exchange(nb_sent, nb_held, to_back, back_sems, g, s)
     for n in (0, 6, 7):
         loads[n].wait()
     interpolate(bg_vel, bg_cells, bg_weights, bg_sent, table, lambda i: None)
     for n in (1, 8, 9):
         loads[n].wait()
-    pl.semaphore_wait(barrier, 127)
-    near_first()
-    interpolate(nb_vel, nb_cells, nb_weights, nb_sent, table, near_some)
+    pl.semaphore_wait(barrier, 22)
+    near.first_hop()
+    interpolate(nb_vel, nb_cells, nb_weights, nb_sent, table, near.second_hop)
     for n in (10, 11, 2, 3, 4, 5):
         loads[n].wait()
-    back_first()
-    near = all_of(bg_sent, to_near, near_sems, me)
-    near.wait_recv()
-    overwrite(nb_vel, nb_rec, to_near, nb_run.at[0], nb_frozen, total, back_some)
+    back.first_hop()
+    near.arrive()
+    overwrite(nb_vel, nb_rec, to_near, nb_run.at[0], nb_frozen, total, back.second_hop)
 
     copies = []
 
@@ -360,8 +387,7 @@
 
     fill_edges(1, 0, nb_run, edge)
     nb_moving = exchange(1, 0, nb_run)
-    back = all_of(nb_sent, to_back, back_sems, me)
-    back.wait_recv()
+    back.arrive()
     overwrite(bg_vel, bg_rec, to_back, bg_run.at[0], bg_frozen, total, lambda i: None)
     fill_edges(0, 0, bg_run, edge)
     moving = [exchange(0, 0, bg_run), nb_moving]
@@ -388,8 +414,8 @@
             if k < SWEEPS - 1:
                 moving[grid] = exchange(grid, k + 1, run)
 
-    near.wait_send()
-    back.wait_send()
+    near.finish()
+    back.finish()
     for copy in copies:
         copy.wait_send()
 
@@ -406,10 +432,12 @@
         + [
             vmem((1536, 256), BF),
             vmem((768, 256), F32),
-            vmem((128, 4, 128), F32),
-            vmem((128, 4, 128), F32),
-            vmem((128, 4, 128), F32),
-            vmem((128, 4, 128), F32),
+            vmem((8, 16, 4, 128), F32),
+            vmem((8, 16, 4, 128), F32),
+            vmem((8, 16, 4, 128), F32),
+            vmem((8, 16, 4, 128), F32),
+            vmem((16, 8, 4, 128), F32),
+            vmem((16, 8, 4, 128), F32),
             vmem((SWEEPS, 3, 10, 16, 256), F32),
             vmem((SWEEPS, 3, 10, 16, 256), F32),
             vmem((8, 16, 256), F32),
@@ -422,8 +450,8 @@
             vmem((2, SWEEPS, 2, 3, 8, 256), F32),
             vmem((2, 2, 8, 256), F32),
             pltpu.SemaphoreType.DMA((12,)),
-            pltpu.SemaphoreType.DMA((2,)),
-            pltpu.SemaphoreType.DMA((2,)),
+            pltpu.SemaphoreType.DMA((4,)),
+            pltpu.SemaphoreType.DMA((4,)),
             pltpu.SemaphoreType.DMA((2, SWEEPS, 4)),
             pltpu.SemaphoreType.DMA((2, SWEEPS, 4)),
         ],

time: 92.6 us -> 83.7 us (0.904)
  Pallas kernels: 89 us -> 80.3 us
    pallas_call x1, Pallas kernels: 89 us -> 80.3 us  [body(): pl.pallas_call(kernel, out_shape=(out, out), in_specs=[pl.BlockSpec(memor...]
where the time goes in v4:
time: 83.7 us; the launch traced here: 83.5 us
  Pallas kernels  80.3 us (96%)
  local copies, waits for them, and re-layouts  2.57 us (3%)
    pallas_call x1, Pallas kernels, body(): pl.pallas_call(kernel, out_shape=(out, out), in_specs=[pl.BlockSpec(memor...  80.3 us
    unnamed x4, local copies, waits for them, and re-layouts  2.57 us

profile of v4, /device:TPU:0, one launch (start us, length us, event | category | flops | bytes accessed | tf_op | source)
XLA Modules:
  0.0 83.5 jit_solution(7063398686521786263)
XLA Ops:
  0.6 80.3 %overset.1 = (f32[3,8,16,256]{3,2,1,0:T(8,128)}, f32[3,8,16,256]{3,2,1,0:T(8,128)}) custom-call(f32[3,8,16,256]{3,2,1,0:T(8,128)} %refs_0_.1, f32[3,8,16,256]{3,2,1,0:T(8,128)} %refs_1_.1, f32[3,8,16,256]{3,2,1,0:T(8,128)} %refs_2_.1, f32[3,8,16,256]{3,2,1,0:T(8,128)} %refs_3_.1, f32[8,16,256]{2,1,0:T(8,128)} %refs_4_.1, f32[8,16,256]{2,1,0:T(8,128)} %refs_5_.1, ...), custom_call_target="tpu_custom_call" | custom-call | tf_op jit(solution)/shard_map/overset/pallas_call | solution.py:426
  81.0 0.0 copy-start
  81.0 1.8 %copy.16 = f32[3,8,16,256]{3,2,1,0:T(8,128)} copy(f32[3,8,16,256]{3,2,1,0:T(8,128)} %get-tuple-element.4) | data formatting | bytes 786432
  82.8 0.0 copy-done
  82.8 0.7 copy.17
Async XLA Ops:
  81.0 1.8 %copy-start = (f32[3,8,16,256]{3,2,1,0:T(8,128)S(1)}, f32[3,8,16,256]{3,2,1,0:T(8,128)}, u32[]{:S(2)}) copy-start(f32[3,8,16,256]{3,2,1,0:T(8,128)} %get-tuple-element.5) | copy-start | bytes 1179652

commit v5 on v4

--- a/solution.py
+++ b/solution.py
@@ -7,6 +7,9 @@
 
 BF = jnp.bfloat16
 F32 = jnp.float32
+F8 = jnp.float8_e4m3fn
+LOW = 256.0
+TINY = 1e-30
 MESH = pl.DeviceIdType.MESH
 SWEEPS = 4
 HOP_STEP = 7
@@ -14,7 +17,7 @@
 
 def split(x):
     hi = x.astype(BF)
-    lo = (x - hi.astype(F32)).astype(BF)
+    lo = ((x - hi.astype(F32)) * LOW).astype(BF)
     return hi, lo
 
 
@@ -22,18 +25,27 @@
     return lax.broadcasted_iota(jnp.int32, shape, dim)
 
 
-def build_table(field, table):
+def scales(peak):
+    peak = jnp.maximum(jnp.max(jnp.max(peak, axis=0, keepdims=True), axis=1, keepdims=True), 1e-30)
+    return 4.0 / peak, peak * 0.25
+
+
+def build_table(field, high, low, low8):
+    peak = jnp.maximum(jnp.maximum(jnp.abs(field[0]), jnp.abs(field[1])), jnp.abs(field[2]))
+    scale, back = scales(peak.reshape(128, 256))
     for c in range(3):
-        here = field[c].reshape(128, 256)
+        here = field[c].reshape(128, 256) * scale
         for zc, x in enumerate((here, pltpu.roll(here, 255, 1))):
             hi, lo = split(x)
             for xx in range(8):
                 at = xx * 96 + zc * 48 + c * 16
-                table[at : at + 16, :] = hi[xx * 16 : xx * 16 + 16]
-                table[768 + at : 784 + at, :] = lo[xx * 16 : xx * 16 + 16]
-
-
-def interpolate_tile(t, cells, weights, out, table):
+                high[at : at + 16, :] = hi[xx * 16 : xx * 16 + 16]
+                low[at : at + 16, :] = lo[xx * 16 : xx * 16 + 16]
+    low8[...] = low[...].astype(F8)
+    return back
+
+
+def interpolate_tile(t, cells, weights, out, high, low8, back):
     z_iota = iota((256, 128), 0).astype(F32).astype(BF)
     y_iota = iota((16, 128), 0)
     tile = cells[0, pl.ds(pl.multiple_of(t * 8, 8), 8), :]
@@ -46,8 +58,9 @@
             for s in (2 * pair, 2 * pair + 1)
         ]
         hot = jnp.concatenate(hot, axis=1)
-        got = jnp.dot(table[0:768, :], hot, preferred_element_type=F32)
-        got = got + jnp.dot(table[768:1536, :], hot, preferred_element_type=F32)
+        hot8 = (hot * (1.0 / LOW)).astype(F8)
+        got = jnp.dot(high[...], hot, preferred_element_type=F32)
+        got = got + jnp.dot(low8[...], hot8, preferred_element_type=F32)
         for half in range(2):
             s = 2 * pair + half
             w = weights[0, t * 8 + s]
@@ -78,15 +91,16 @@
                         acc[c] = term if acc[c] is None else acc[c] + term
                 before = here
             for c in range(3):
-                out[t // 2, (t % 2) * 8 + s, c, :] = jnp.sum(acc[c], axis=0)
-
-
-def interpolate(field, cells, weights, sent, table, beside):
-    build_table(field, table)
+                out[t // 2, (t % 2) * 8 + s, c, :] = jnp.sum(acc[c], axis=0) * back[0]
+
+
+def interpolate(field, cells, weights, sent, tables, beside):
+    high, low, low8 = tables
+    back = build_table(field, high, low, low8)
 
     def step(i, carry):
         beside(i)
-        interpolate_tile(i, cells, weights, sent, table)
+        interpolate_tile(i, cells, weights, sent, high, low8, back)
         return carry
 
     lax.fori_loop(0, 16, step, 0)
@@ -162,7 +176,11 @@
 def overwrite(field, receptors, got, start, frozen, total, beside):
     z_iota = iota((256, 128), 0).astype(F32).astype(BF)
     r_iota = iota((128, 128), 0).astype(F32).astype(BF)
-    lift = jnp.where(iota((4, 128), 0) == 0, 8.0, 0.0)
+    row = iota((4, 128), 0)
+    peak = jnp.zeros((4, 128), F32)
+    for p in range(16):
+        peak = jnp.maximum(peak, jnp.max(jnp.abs(got[p]), axis=0))
+    scale, back = scales(jnp.where(row < 3, peak, 0.0))
     one = jnp.ones((), BF)
     zero = jnp.zeros((), BF)
     total[...] = jnp.zeros_like(total)
@@ -174,30 +192,39 @@
         r_tile = (tile >> 8).astype(F32).astype(BF)
         for half in range(2):
             hots = []
-            lefts = []
+            highs = []
+            lows = []
             for s in range(4 * half, 4 * half + 4):
                 hots.append(jnp.where(z_iota == z_tile[s : s + 1, :], one, zero))
                 mine = r_iota == r_tile[s : s + 1, :]
-                parts = split(got[(i % 2) * 8 + s, i // 2] + lift)
-                rows = [jnp.where(mine, p[c : c + 1, :], zero) for p in parts for c in range(3)]
-                lefts.append(jnp.concatenate(rows, axis=0))
+                hi, lo = split(got[(i % 2) * 8 + s, i // 2] * scale)
+                hi = hi.astype(F32)
+                hi = jnp.where((hi == 0.0) & (row == 0), TINY, hi).astype(BF)
+                for rows, part in ((highs, hi), (lows, lo)):
+                    picked = [jnp.where(mine, part[c : c + 1, :], zero) for c in range(3)]
+                    rows.append(jnp.concatenate(picked, axis=0))
+            hot = jnp.concatenate(hots, axis=1)
+            hot8 = (hot * (1.0 / LOW)).astype(F8)
+            over_slots = (((1,), (1,)), ((), ()))
             total[...] += lax.dot_general(
-                jnp.concatenate(lefts, axis=1),
-                jnp.concatenate(hots, axis=1),
-                (((1,), (1,)), ((), ())),
+                jnp.concatenate(highs, axis=1), hot, over_slots, preferred_element_type=F32
+            ) + lax.dot_general(
+                jnp.concatenate(lows, axis=1).astype(F8),
+                hot8,
+                over_slots,
                 preferred_element_type=F32,
             )
         return carry
 
     lax.fori_loop(0, 16, step, 0)
-    mask = total[0:128, :]
-    frozen[...] = mask.reshape(8, 16, 256)
+    mask = total[0:128, :] != 0.0
+    frozen[...] = jnp.where(mask, 1.0, 0.0).reshape(8, 16, 256)
     for c in range(3):
-        value = total[c * 128 : c * 128 + 128, :] + total[384 + c * 128 : 512 + c * 128, :]
+        value = total[c * 128 : c * 128 + 128, :]
         if c == 0:
-            value = value - 8.0
+            value = jnp.where(jnp.abs(value) < 2.0 * TINY, 0.0, value)
         old = field[c].reshape(128, 256)
-        start[c, 1:9] = jnp.where(mask > 1.0, value, old).reshape(8, 16, 256)
+        start[c, 1:9] = jnp.where(mask, value * back, old).reshape(8, 16, 256)
 
 
 def halo_copies(grid, k, velocity, edge, halo, send_sems, recv_sems, g, s):
@@ -272,7 +299,7 @@
         for f in faces:
             diagonal = diagonal + f
         inverse = 1.0 / diagonal
-        stuck = frozen[x] > 1.0
+        stuck = frozen[x] > 0.5
         live = jnp.where(stuck, 0.0, inverse)
         faces = [f * live for f in faces]
         coef[0, x] = faces[0] * x_high
@@ -330,7 +357,7 @@
         bg_out, nb_out,
         bg_vel, nb_vel, bg_source, nb_source, bg_inertia, nb_inertia,
         bg_cells, bg_weights, nb_cells, nb_weights, nb_rec, bg_rec,
-        table, total,
+        high, low, low8, total,
         bg_sent, nb_sent, bg_held, nb_held, to_near, to_back, bg_run, nb_run,
         bg_frozen, nb_frozen, bg_coef, nb_coef, bg_rhs, nb_rhs, edge, halo, rim,
         load_sems, near_sems, back_sems, send_sems, recv_sems,
@@ -364,12 +391,12 @@
     back = Exchange(nb_sent, nb_held, to_back, back_sems, g, s)
     for n in (0, 6, 7):
         loads[n].wait()
-    interpolate(bg_vel, bg_cells, bg_weights, bg_sent, table, lambda i: None)
+    interpolate(bg_vel, bg_cells, bg_weights, bg_sent, (high, low, low8), lambda i: None)
     for n in (1, 8, 9):
         loads[n].wait()
     pl.semaphore_wait(barrier, 22)
     near.first_hop()
-    interpolate(nb_vel, nb_cells, nb_weights, nb_sent, table, near.second_hop)
+    interpolate(nb_vel, nb_cells, nb_weights, nb_sent, (high, low, low8), near.second_hop)
     for n in (10, 11, 2, 3, 4, 5):
         loads[n].wait()
     back.first_hop()
@@ -430,8 +457,10 @@
         out_specs=[pl.BlockSpec(memory_space=vmem)] * 2,
         scratch_shapes=[vmem(a.shape, a.dtype) for a in args]
         + [
-            vmem((1536, 256), BF),
-            vmem((768, 256), F32),
+            vmem((768, 256), BF),
+            vmem((768, 256), BF),
+            vmem((768, 256), F8),
+            vmem((384, 256), F32),
             vmem((8, 16, 4, 128), F32),
             vmem((8, 16, 4, 128), F32),
             vmem((8, 16, 4, 128), F32),

time: 83.7 us -> 78.3 us (0.935)
  Pallas kernels: 80.3 us -> 75 us
    pallas_call x1, Pallas kernels: 80.3 us -> 75 us  [body(): pl.pallas_call(kernel, out_shape=(out, out), in_specs=[pl.BlockSpec(memor...]
where the time goes in v5:
time: 78.3 us; the launch traced here: 78.2 us
  Pallas kernels  75 us (96%)
  local copies, waits for them, and re-layouts  2.57 us (3%)
    pallas_call x1, Pallas kernels, body(): pl.pallas_call(kernel, out_shape=(out, out), in_specs=[pl.BlockSpec(memor...  75 us
    unnamed x4, local copies, waits for them, and re-layouts  2.57 us

profile of v5, /device:TPU:0, one launch (start us, length us, event | category | flops | bytes accessed | tf_op | source)
XLA Modules:
  0.0 78.2 jit_solution(4244223815056267458)
XLA Ops:
  0.6 75.0 %overset.1 = (f32[3,8,16,256]{3,2,1,0:T(8,128)}, f32[3,8,16,256]{3,2,1,0:T(8,128)}) custom-call(f32[3,8,16,256]{3,2,1,0:T(8,128)} %refs_0_.1, f32[3,8,16,256]{3,2,1,0:T(8,128)} %refs_1_.1, f32[3,8,16,256]{3,2,1,0:T(8,128)} %refs_2_.1, f32[3,8,16,256]{3,2,1,0:T(8,128)} %refs_3_.1, f32[8,16,256]{2,1,0:T(8,128)} %refs_4_.1, f32[8,16,256]{2,1,0:T(8,128)} %refs_5_.1, ...), custom_call_target="tpu_custom_call" | custom-call | tf_op jit(solution)/shard_map/overset/pallas_call | solution.py:453
  75.6 0.0 copy-start
  75.6 1.8 %copy.16 = f32[3,8,16,256]{3,2,1,0:T(8,128)} copy(f32[3,8,16,256]{3,2,1,0:T(8,128)} %get-tuple-element.4) | data formatting | bytes 786432
  77.4 0.0 copy-done
  77.4 0.7 copy.17
Async XLA Ops:
  75.6 1.8 %copy-start = (f32[3,8,16,256]{3,2,1,0:T(8,128)S(1)}, f32[3,8,16,256]{3,2,1,0:T(8,128)}, u32[]{:S(2)}) copy-start(f32[3,8,16,256]{3,2,1,0:T(8,128)} %get-tuple-element.5) | copy-start | bytes 1179652

commit v6 on v5

--- a/solution.py
+++ b/solution.py
@@ -1,3 +1,5 @@
+import functools
+
 import jax
 import jax.numpy as jnp
 from jax import lax
@@ -370,11 +372,17 @@
     loads = [
         pltpu.make_async_copy(hbm[n], vmem[n], load_sems.at[n]) for n in range(12)
     ]
-    for n in (0, 6, 7, 1, 8, 9, 10, 11, 2, 3, 4, 5):
+    for n in (0, 6, 7):
         loads[n].start()
 
     barrier = pltpu.get_barrier_semaphore()
 
+    for c in range(3):
+        for end in (0, 9):
+            nb_run[0, c, end] = jnp.zeros((16, 256), F32)
+            for k in range(SWEEPS):
+                bg_run[k, c, end] = jnp.zeros((16, 256), F32)
+    halo[...] = jnp.zeros_like(halo)
     for offset in range(1, 8):
         pl.semaphore_signal(
             barrier, inc=1, device_id=((g + offset) % 8, s), device_id_type=MESH
@@ -383,14 +391,13 @@
         pl.semaphore_signal(
             barrier, inc=1, device_id=(g, (s + offset) % 16), device_id_type=MESH
         )
-    for c in range(3):
-        nb_run[0, c, 0] = jnp.zeros((16, 256), F32)
-        nb_run[0, c, 9] = jnp.zeros((16, 256), F32)
 
     near = Exchange(bg_sent, bg_held, to_near, near_sems, g, s)
     back = Exchange(nb_sent, nb_held, to_back, back_sems, g, s)
     for n in (0, 6, 7):
         loads[n].wait()
+    for n in (1, 8, 9, 10, 11, 2, 3, 4, 5):
+        loads[n].start()
     interpolate(bg_vel, bg_cells, bg_weights, bg_sent, (high, low, low8), lambda i: None)
     for n in (1, 8, 9):
         loads[n].wait()
@@ -403,13 +410,18 @@
     near.arrive()
     overwrite(nb_vel, nb_rec, to_near, nb_run.at[0], nb_frozen, total, back.second_hop)
 
+    goes = (s < 15, s > 0, g < 7, g > 0)
+    comes = (s > 0, s < 15, g > 0, g < 7)
     copies = []
+
+    def each(conditions, new, act):
+        for condition, copy in zip(conditions, new):
+            pl.when(condition)(functools.partial(act, copy))
 
     def exchange(grid, k, velocity):
         new = halo_copies(grid, k, velocity, edge, halo, send_sems, recv_sems, g, s)
-        for copy in new:
-            copy.start()
-        copies.extend(new)
+        each(goes, new, lambda copy: copy.start())
+        copies.append(new)
         return new
 
     fill_edges(1, 0, nb_run, edge)
@@ -430,21 +442,19 @@
             now = run.at[k]
             after = run.at[k + 1, :, pl.ds(1, 8)] if k < SWEEPS - 1 else outs[grid]
             if k == 0:
-                for copy in moving[grid]:
-                    copy.wait_recv()
+                each(comes, moving[grid], lambda copy: copy.wait_recv())
                 assemble(grid, run, halo, *fields[grid], coef, rhs, rim, g, s)
             inner(now, coef, rhs, after)
             if k > 0:
-                for copy in moving[grid]:
-                    copy.wait_recv()
+                each(comes, moving[grid], lambda copy: copy.wait_recv())
             outer(grid, k, now, halo, coef, rim, after, edge)
             if k < SWEEPS - 1:
                 moving[grid] = exchange(grid, k + 1, run)
 
     near.finish()
     back.finish()
-    for copy in copies:
-        copy.wait_send()
+    for new in copies:
+        each(goes, new, lambda copy: copy.wait_send())
 
 
 def body(*args):

time: 78.3 us -> 75.1 us (0.959)
  the two profiles are of different devices: /device:TPU:0 before, /device:TPU:32 now
where the time goes in v6:
time: 75.1 us; the launch traced here: 74.9 us
  Pallas kernels  71.7 us (95%)
  local copies, waits for them, and re-layouts  2.57 us (3%)
    pallas_call x1, Pallas kernels, body(): pl.pallas_call(kernel, out_shape=(out, out), in_specs=[pl.BlockSpec(memor...  71.7 us
    unnamed x4, local copies, waits for them, and re-layouts  2.57 us

profile of v6, /device:TPU:32, one launch (start us, length us, event | category | flops | bytes accessed | tf_op | source)
XLA Modules:
  0.0 74.9 jit_solution(11431855719048721855)
XLA Ops:
  0.6 71.7 %overset.1 = (f32[3,8,16,256]{3,2,1,0:T(8,128)}, f32[3,8,16,256]{3,2,1,0:T(8,128)}) custom-call(f32[3,8,16,256]{3,2,1,0:T(8,128)} %refs_0_.1, f32[3,8,16,256]{3,2,1,0:T(8,128)} %refs_1_.1, f32[3,8,16,256]{3,2,1,0:T(8,128)} %refs_2_.1, f32[3,8,16,256]{3,2,1,0:T(8,128)} %refs_3_.1, f32[8,16,256]{2,1,0:T(8,128)} %refs_4_.1, f32[8,16,256]{2,1,0:T(8,128)} %refs_5_.1, ...), custom_call_target="tpu_custom_call" | custom-call | tf_op jit(solution)/shard_map/overset/pallas_call | solution.py:463
  72.3 0.0 copy-start
  72.3 1.8 %copy.16 = f32[3,8,16,256]{3,2,1,0:T(8,128)} copy(f32[3,8,16,256]{3,2,1,0:T(8,128)} %get-tuple-element.4) | data formatting | bytes 786432
  74.2 0.0 copy-done
  74.2 0.7 copy.17
Async XLA Ops:
  72.3 1.8 %copy-start = (f32[3,8,16,256]{3,2,1,0:T(8,128)S(1)}, f32[3,8,16,256]{3,2,1,0:T(8,128)}, u32[]{:S(2)}) copy-start(f32[3,8,16,256]{3,2,1,0:T(8,128)} %get-tuple-element.5) | copy-start | bytes 1179652

commit v7 on v6

--- a/solution.py
+++ b/solution.py
@@ -10,16 +10,15 @@
 BF = jnp.bfloat16
 F32 = jnp.float32
 F8 = jnp.float8_e4m3fn
-LOW = 256.0
+REACH = 1024.0
 TINY = 1e-30
 MESH = pl.DeviceIdType.MESH
 SWEEPS = 4
-HOP_STEP = 7
 
 
 def split(x):
     hi = x.astype(BF)
-    lo = ((x - hi.astype(F32)) * LOW).astype(BF)
+    lo = (x - hi.astype(F32)).astype(BF)
     return hi, lo
 
 
@@ -29,7 +28,7 @@
 
 def scales(peak):
     peak = jnp.maximum(jnp.max(jnp.max(peak, axis=0, keepdims=True), axis=1, keepdims=True), 1e-30)
-    return 4.0 / peak, peak * 0.25
+    return REACH / peak, peak * (1.0 / REACH)
 
 
 def build_table(field, high, low, low8):
@@ -60,7 +59,7 @@
             for s in (2 * pair, 2 * pair + 1)
         ]
         hot = jnp.concatenate(hot, axis=1)
-        hot8 = (hot * (1.0 / LOW)).astype(F8)
+        hot8 = hot.astype(F8)
         got = jnp.dot(high[...], hot, preferred_element_type=F32)
         got = got + jnp.dot(low8[...], hot8, preferred_element_type=F32)
         for half in range(2):
@@ -109,8 +108,9 @@
 
 
 class Exchange:
-    def __init__(self, sent, held, came, sems, g, s):
+    def __init__(self, sent, held, came, sems, g, s, turn):
         self.sent, self.held, self.came, self.sems, self.g, self.s = sent, held, came, sems, g, s
+        self.turn = turn
 
     def across(self, offset):
         peer = (self.g + offset) % 8
@@ -160,7 +160,7 @@
         self.held[self.g] = self.sent[self.g]
 
     def second_hop(self, i):
-        @pl.when(i == HOP_STEP)
+        @pl.when(i == self.turn)
         def _():
             self.all_across().wait_recv()
             for offset in range(1, 16):
@@ -206,7 +206,7 @@
                     picked = [jnp.where(mine, part[c : c + 1, :], zero) for c in range(3)]
                     rows.append(jnp.concatenate(picked, axis=0))
             hot = jnp.concatenate(hots, axis=1)
-            hot8 = (hot * (1.0 / LOW)).astype(F8)
+            hot8 = hot.astype(F8)
             over_slots = (((1,), (1,)), ((), ()))
             total[...] += lax.dot_general(
                 jnp.concatenate(highs, axis=1), hot, over_slots, preferred_element_type=F32
@@ -315,7 +315,7 @@
             rhs[c, x] = jnp.where(stuck, start, right)
         return carry
 
-    lax.fori_loop(0, 8, step, 0)
+    lax.fori_loop(0, 8, step, 0, unroll=4)
     rim[grid, 0] = coef[3, :, 0, :] * y_low
     rim[grid, 1] = coef[2, :, 15, :] * y_high
     coef[3, :, 0, :] = jnp.zeros((8, 256), F32)
@@ -392,8 +392,8 @@
             barrier, inc=1, device_id=(g, (s + offset) % 16), device_id_type=MESH
         )
 
-    near = Exchange(bg_sent, bg_held, to_near, near_sems, g, s)
-    back = Exchange(nb_sent, nb_held, to_back, back_sems, g, s)
+    near = Exchange(bg_sent, bg_held, to_near, near_sems, g, s, 7)
+    back = Exchange(nb_sent, nb_held, to_back, back_sems, g, s, 5)
     for n in (0, 6, 7):
         loads[n].wait()
     for n in (1, 8, 9, 10, 11, 2, 3, 4, 5):

time: 75.1 us -> 74 us (0.985)
  Pallas kernels: 71.7 us -> 70.7 us
    pallas_call x1, Pallas kernels: 71.7 us -> 70.7 us  [body(): pl.pallas_call(kernel, out_shape=(out, out), in_specs=[pl.BlockSpec(memor...]
where the time goes in v7:
time: 74 us; the launch traced here: 73.9 us
  Pallas kernels  70.7 us (96%)
  local copies, waits for them, and re-layouts  2.57 us (3%)
    pallas_call x1, Pallas kernels, body(): pl.pallas_call(kernel, out_shape=(out, out), in_specs=[pl.BlockSpec(memor...  70.7 us
    unnamed x4, local copies, waits for them, and re-layouts  2.57 us

profile of v7, /device:TPU:32, one launch (start us, length us, event | category | flops | bytes accessed | tf_op | source)
XLA Modules:
  0.0 73.9 jit_solution(6063364734423624263)
XLA Ops:
  0.6 70.7 %overset.1 = (f32[3,8,16,256]{3,2,1,0:T(8,128)}, f32[3,8,16,256]{3,2,1,0:T(8,128)}) custom-call(f32[3,8,16,256]{3,2,1,0:T(8,128)} %refs_0_.1, f32[3,8,16,256]{3,2,1,0:T(8,128)} %refs_1_.1, f32[3,8,16,256]{3,2,1,0:T(8,128)} %refs_2_.1, f32[3,8,16,256]{3,2,1,0:T(8,128)} %refs_3_.1, f32[8,16,256]{2,1,0:T(8,128)} %refs_4_.1, f32[8,16,256]{2,1,0:T(8,128)} %refs_5_.1, ...), custom_call_target="tpu_custom_call" | custom-call | tf_op jit(solution)/shard_map/overset/pallas_call | solution.py:463
  71.3 0.0 copy-start
  71.3 1.8 %copy.16 = f32[3,8,16,256]{3,2,1,0:T(8,128)} copy(f32[3,8,16,256]{3,2,1,0:T(8,128)} %get-tuple-element.4) | data formatting | bytes 786432
  73.1 0.0 copy-done
  73.1 0.7 %copy.17 = f32[3,8,16,256]{3,2,1,0:T(8,128)} copy(f32[3,8,16,256]{3,2,1,0:T(8,128)S(1)} %copy-done) | data formatting | bytes 786432
Async XLA Ops:
  71.3 1.8 %copy-start = (f32[3,8,16,256]{3,2,1,0:T(8,128)S(1)}, f32[3,8,16,256]{3,2,1,0:T(8,128)}, u32[]{:S(2)}) copy-start(f32[3,8,16,256]{3,2,1,0:T(8,128)} %get-tuple-element.5) | copy-start | bytes 1179652

commit v8 on v7

--- a/solution.py
+++ b/solution.py
@@ -95,9 +95,10 @@
                 out[t // 2, (t % 2) * 8 + s, c, :] = jnp.sum(acc[c], axis=0) * back[0]
 
 
-def interpolate(field, cells, weights, sent, tables, beside):
+def interpolate(field, cells, weights, sent, tables, ready, beside):
     high, low, low8 = tables
     back = build_table(field, high, low, low8)
+    ready()
 
     def step(i, carry):
         beside(i)
@@ -394,16 +395,19 @@
 
     near = Exchange(bg_sent, bg_held, to_near, near_sems, g, s, 7)
     back = Exchange(nb_sent, nb_held, to_back, back_sems, g, s, 5)
-    for n in (0, 6, 7):
-        loads[n].wait()
-    for n in (1, 8, 9, 10, 11, 2, 3, 4, 5):
-        loads[n].start()
-    interpolate(bg_vel, bg_cells, bg_weights, bg_sent, (high, low, low8), lambda i: None)
+    def bg_ready():
+        for n in (6, 7):
+            loads[n].wait()
+        for n in (1, 8, 9, 10, 11, 2, 3, 4, 5):
+            loads[n].start()
+
+    loads[0].wait()
+    interpolate(bg_vel, bg_cells, bg_weights, bg_sent, (high, low, low8), bg_ready, lambda i: None)
     for n in (1, 8, 9):
         loads[n].wait()
     pl.semaphore_wait(barrier, 22)
     near.first_hop()
-    interpolate(nb_vel, nb_cells, nb_weights, nb_sent, (high, low, low8), near.second_hop)
+    interpolate(nb_vel, nb_cells, nb_weights, nb_sent, (high, low, low8), lambda: None, near.second_hop)
     for n in (10, 11, 2, 3, 4, 5):
         loads[n].wait()
     back.first_hop()

time: 74 us -> 73.8 us (level)
  no operation moved by 1% of the time
where the time goes in v8:
time: 73.8 us; the launch traced here: 73.7 us
  Pallas kernels  70.5 us (96%)
  local copies, waits for them, and re-layouts  2.57 us (3%)
    pallas_call x1, Pallas kernels, body(): pl.pallas_call(kernel, out_shape=(out, out), in_specs=[pl.BlockSpec(memor...  70.5 us
    unnamed x4, local copies, waits for them, and re-layouts  2.57 us

profile of v8, /device:TPU:32, one launch (start us, length us, event | category | flops | bytes accessed | tf_op | source)
XLA Modules:
  0.0 73.7 jit_solution(11862800253083549336)
XLA Ops:
  0.6 70.5 %overset.1 = (f32[3,8,16,256]{3,2,1,0:T(8,128)}, f32[3,8,16,256]{3,2,1,0:T(8,128)}) custom-call(f32[3,8,16,256]{3,2,1,0:T(8,128)} %refs_0_.1, f32[3,8,16,256]{3,2,1,0:T(8,128)} %refs_1_.1, f32[3,8,16,256]{3,2,1,0:T(8,128)} %refs_2_.1, f32[3,8,16,256]{3,2,1,0:T(8,128)} %refs_3_.1, f32[8,16,256]{2,1,0:T(8,128)} %refs_4_.1, f32[8,16,256]{2,1,0:T(8,128)} %refs_5_.1, ...), custom_call_target="tpu_custom_call" | custom-call | tf_op jit(solution)/shard_map/overset/pallas_call | solution.py:467
  71.1 0.0 copy-start
  71.1 1.8 %copy.16 = f32[3,8,16,256]{3,2,1,0:T(8,128)} copy(f32[3,8,16,256]{3,2,1,0:T(8,128)} %get-tuple-element.4) | data formatting | bytes 786432
  72.9 0.0 copy-done
  72.9 0.7 %copy.17 = f32[3,8,16,256]{3,2,1,0:T(8,128)} copy(f32[3,8,16,256]{3,2,1,0:T(8,128)S(1)} %copy-done) | data formatting | bytes 786432
Async XLA Ops:
  71.1 1.8 %copy-start = (f32[3,8,16,256]{3,2,1,0:T(8,128)S(1)}, f32[3,8,16,256]{3,2,1,0:T(8,128)}, u32[]{:S(2)}) copy-start(f32[3,8,16,256]{3,2,1,0:T(8,128)} %get-tuple-element.5) | copy-start | bytes 1179652
